TPU v7x, 512 devices: a whole 4x8x8 slice. The times are simulated.
512 devices in a mesh: prompt: 8 (over y), roll: 16 (over x, z_lo, core), head: 4 (over z_hi).
Axes of the slice: x: 4, y: 8, z: 8 (z_hi: 4, z_lo: 2; z = z_hi * 2 + z_lo), core: 2. Of those that a mesh axis runs over, the one named last changes fastest.
Arguments:
- queries: bfloat16 [128, 128, 4096], P(('prompt', 'roll'), None, 'head'), parts along dimension 0, may hold values from -100 to 100
- resp_keys: bfloat16 [128, 128, 512], P(('prompt', 'roll'), None, 'head'), parts along dimension 0, may hold values from -6 to 6
- resp_values: bfloat16 [128, 128, 512], P(('prompt', 'roll'), None, 'head'), parts along dimension 0, may hold values from -6 to 6
- prefix_keys: bfloat16 [8192, 512], P(('prompt', 'roll'), 'head'), parts along dimension 0, may hold values from -4.1 to 4.1
- prefix_values: bfloat16 [8192, 512], P(('prompt', 'roll'), 'head'), parts along dimension 0, may hold values from -6 to 6
- grad_out: bfloat16 [128, 128, 4096], P(('prompt', 'roll'), None, 'head'), parts along dimension 0, may hold values from -6 to 6
- lengths: int32 [128], P(('prompt', 'roll')), parts along dimension 0, may hold values from 1 to 128, 1024 in all
Outputs:
- attended: bfloat16 [128, 128, 4096], P(('prompt', 'roll'), None, 'head'), parts along dimension 0
- query_grad: bfloat16 [128, 128, 4096], P(('prompt', 'roll'), None, 'head'), parts along dimension 0
- key_grad: bfloat16 [128, 128, 512], P(('prompt', 'roll'), None, 'head'), parts along dimension 0
- value_grad: bfloat16 [128, 128, 512], P(('prompt', 'roll'), None, 'head'), parts along dimension 0
- shared_key_grad: float32 [8192, 512], P(('prompt', 'roll'), 'head'), parts along dimension 0
- shared_value_grad: float32 [8192, 512], P(('prompt', 'roll'), 'head'), parts along dimension 0
There are 8 independent parts, one for each index of `prompt`. A program takes and returns all parts, laid end to end along the dimension named above; each array names one. Nothing has to cross between parts.
Inputs may be any that keep to these rules, and one draw needn't show every extreme that they name: `lengths`: the longest rollout of every prompt has exactly 128 live tokens.
All inputs are finite; a program needn't handle non-finite values. No bound on the sum of `lengths` on one device may be relied on, other than what follows from the above.
Results may differ from a plain program's by a relative error of at most 0.009.
Values may be sent and summed in bfloat16 or wider, within the bound.
No kernel may reach another device: no remote copies, remote signals or barrier semaphores. Data moves between devices by JAX's collectives and lax.ppermute only.
A program may use at most 64 MiB of HBM per device.

v0:
```python
import math

import jax
import jax.numpy as jnp
from jax import lax
from jax.sharding import PartitionSpec as P

masked_score = -1e30


def contract_last(left, right):
    return lax.dot_general(
        left, right, (((1,), (1,)), ((), ())), preferred_element_type=jnp.float32
    )


def contract_first(left, right):
    return lax.dot_general(
        left, right, (((0,), (0,)), ((), ())), preferred_element_type=jnp.float32
    )


def on_device(queries, resp_keys, resp_values, prefix_keys, prefix_values, grad_out, lengths):
    tokens = queries.shape[1]
    head_size = resp_keys.shape[2]
    group_size = queries.shape[2] // head_size
    length = lengths[0]
    factor = 1.0 / math.sqrt(head_size)
    shared_keys, shared_values = (
        lax.all_gather(prefix_keys, "roll", axis=0, tiled=True),
        lax.all_gather(prefix_values, "roll", axis=0, tiled=True),
    )
    prompt = shared_keys.shape[0]
    key_rows = jnp.concatenate([shared_keys, resp_keys[0]], axis=0)
    value_rows = jnp.concatenate([shared_values, resp_values[0]], axis=0)
    stride = min(tokens, 64)
    row_count = stride * group_size
    key_index = jnp.arange(prompt + tokens, dtype=jnp.int32)[None, :] - prompt
    summed_rows = prompt + tokens
    key_sum = jnp.zeros((summed_rows, head_size), jnp.float32)
    value_sum = jnp.zeros((summed_rows, head_size), jnp.float32)
    attended_parts = []
    query_parts = []
    for offset in range(0, tokens, stride):
        query_rows = queries[0, offset : offset + stride].reshape(row_count, head_size)
        token_index = offset + jnp.arange(row_count, dtype=jnp.int32)[:, None] // group_size
        living = token_index < length
        grad_rows = grad_out[0, offset : offset + stride].reshape(row_count, head_size)
        grad_rows = jnp.where(living, grad_rows, jnp.zeros_like(grad_rows))
        allowed = (key_index < 0) | (key_index <= token_index) & (key_index < length)
        scores = jnp.where(allowed, contract_last(query_rows, key_rows) * factor, masked_score)
        row_max = jnp.max(scores, axis=1, keepdims=True)
        exponent = jnp.exp(scores - row_max)
        denominator = jnp.sum(exponent, axis=1, keepdims=True)
        probability = exponent / denominator
        rounded = probability.astype(jnp.bfloat16)
        outputs = jnp.dot(rounded, value_rows, preferred_element_type=jnp.float32)
        attended_parts.append(
            jnp.where(living, outputs, 0.0)
            .astype(jnp.bfloat16)
            .reshape(stride, group_size * head_size)
        )
        grad_weights = contract_last(grad_rows, value_rows)
        correction = jnp.sum(probability * grad_weights, axis=1, keepdims=True)
        grad_scores = (probability * (grad_weights - correction) * factor).astype(jnp.bfloat16)
        query_value = jnp.dot(grad_scores, key_rows, preferred_element_type=jnp.float32)
        query_parts.append(query_value.astype(jnp.bfloat16).reshape(stride, group_size * head_size))
        key_sum = key_sum + contract_first(grad_scores, query_rows)
        value_sum = value_sum + contract_first(rounded, grad_rows)
    prefix_part = jnp.concatenate([key_sum[:prompt], value_sum[:prompt]], axis=1)
    shares = lax.psum_scatter(prefix_part, "roll", scatter_dimension=0, tiled=True)
    own_keys = key_sum[prompt:]
    own_values = value_sum[prompt:]
    attended = jnp.concatenate(attended_parts, axis=0)[None]
    query_grad = jnp.concatenate(query_parts, axis=0)[None]
    key_grad = own_keys.astype(jnp.bfloat16)[None]
    value_grad = own_values.astype(jnp.bfloat16)[None]
    return (
        attended,
        query_grad,
        key_grad,
        value_grad,
        shares[:, :head_size],
        shares[:, head_size:],
    )


def solution(mesh):
    return jax.shard_map(
        on_device,
        mesh=mesh,
        in_specs=(
            P(("prompt", "roll"), None, "head"),
            P(("prompt", "roll"), None, "head"),
            P(("prompt", "roll"), None, "head"),
            P(("prompt", "roll"), "head"),
            P(("prompt", "roll"), "head"),
            P(("prompt", "roll"), None, "head"),
            P(("prompt", "roll")),
        ),
        out_specs=(
            P(("prompt", "roll"), None, "head"),
            P(("prompt", "roll"), None, "head"),
            P(("prompt", "roll"), None, "head"),
            P(("prompt", "roll"), None, "head"),
            P(("prompt", "roll"), "head"),
            P(("prompt", "roll"), "head"),
        ),
        check_vma=False,
    )
```

profile of v0, /device:TPU:1, one launch (start us, length us, event | category | flops | bytes accessed | tf_op | source)
XLA Modules:
  0.0 137.9 jit_solution(4958656122010017715)
XLA Ops:
  8.0 24.1 %all_gather.6 = bf16[1024,128]{1,0:T(8,128)(2,1)S(1)} all-gather(bf16[64,128]{1,0:T(8,128)(2,1)} %param.10), channel_id=1, replica_groups=mesh['prompt'=8,'roll'=16,'head'=4] {'roll'}, dimensions={0}, use_global_device_ids=true | all-gather | bytes 278528 | tf_op jit(solution)/shard_map/all_gather | solution.py:30
  32.0 19.0 %all_gather.7 = bf16[1024,128]{1,0:T(8,128)(2,1)S(1)} all-gather(bf16[64,128]{1,0:T(8,128)(2,1)} %param.11), channel_id=1, replica_groups=mesh['prompt'=8,'roll'=16,'head'=4] {'roll'}, dimensions={0}, use_global_device_ids=true | all-gather | bytes 278528 | tf_op jit(solution)/shard_map/all_gather | solution.py:31
  51.1 1.1 fusion.33
  52.3 1.0 fusion.32
  53.5 0.8 fusion.35
  54.7 0.8 fusion.36
  56.6 0.7 multiply_reduce_fusion.1
  58.7 0.7 copy-done.4
  62.0 0.8 copy-done.3
  62.9 1.1 pad_maximum_fusion
  64.0 2.5 %copy.31 = f32[1024,256]{1,0:T(8,128)} copy(f32[1024,256]{0,1:T(8,128)} %pad_maximum_fusion) | data formatting | bytes 2097152
  66.6 2.9 %fusion.9 = bf16[512,128]{1,0:T(8,128)(2,1)} fusion(pred[512]{0:T(512)(128)(4,1)} %copy-done.15, bf16[128,128]{1,0:T(8,128)(2,1)} %bitcast.30, bf16[1024,128]{1,0:T(8,128)(2,1)} %copy-done.10, f32[512,1152]{0,1:T(8,128)} %copy-done, f32[512]{0:T(512)S(1)} %fusion.7, f32[512]{0:T(512)S(1)} %get-tuple-element.24), kind=kOutput, calls=%fused_computation.21 | convolution fusion | flops 153485312 | bytes 2789888 | tf_op jit(solution)/shard_map/dot_general | solution.py:57
  69.5 1.6 %reshape.88 = bf16[64,1024]{1,0:T(8,128)(2,1)} reshape(bf16[512,128]{1,0:T(8,128)(2,1)} %fusion.9) | data formatting | bytes 262144 | tf_op jit(solution)/shard_map/reshape | solution.py:61
  71.1 2.2 %fusion.8 = bf16[512,128]{1,0:T(8,128)(2,1)} fusion(pred[512]{0:T(512)(128)(4,1)} %copy-done.14, bf16[128,128]{1,0:T(8,128)(2,1)} %bitcast.31, bf16[1024,128]{1,0:T(8,128)(2,1)} %copy-done.10, f32[512,1152]{0,1:T(8,128)S(1)} %get-tuple-element.27, f32[512]{0:T(512)S(1)} %fusion.5, f32[512]{0:T(512)S(1)} %get-tuple-element.26), kind=kOutput, calls=%fused_computation.20 | convolution fusion | flops 153485312 | bytes 2789888 | tf_op jit(solution)/shard_map/dot_general | solution.py:57
  73.2 1.1 reshape.87
  74.3 0.8 fusion.18
  75.2 0.7 copy.26
  75.9 1.5 %convolution_convert_fusion = bf16[512,128]{1,0:T(8,128)(2,1)S(1)} fusion(bf16[512,1152]{0,1:T(8,128)(2,1)S(1)} %multiply_convert_fusion, bf16[128,128]{1,0:T(8,128)(2,1)} %bitcast.34, bf16[1024,128]{1,0:T(8,128)(2,1)} %copy-done.8), kind=kOutput, calls=%fused_computation.22 | convolution fusion | flops 151650304 | bytes 1605632 | tf_op jit(solution)/shard_map/dot_general | solution.py:66
  78.1 0.8 fusion.17
  78.9 0.7 copy.25
  79.6 0.7 maximum_bitcast_fusion
  80.4 0.7 maximum_bitcast_fusion.1
  81.1 48.6 %reduce-scatter.4.cloned.1.call-done = f32[64,256]{1,0:T(8,128)} async-done(((f32[1024,256]{1,0:T(8,128)}), f32[64,256]{1,0:T(8,128)}) %reduce-scatter.4.cloned.1.call-update) | async-done | bytes 65552
  129.7 1.4 %fusion.34 = (f32[64,128]{1,0:T(8,128)}, f32[64,128]{1,0:T(8,128)}) fusion(f32[64,256]{1,0:T(8,128)} %reduce-scatter.4.cloned.1.call-done), kind=kLoop, calls=%fused_computation.61 | loop fusion | bytes 131072 | tf_op jit(solution)/shard_map/slice | solution.py:84
  (55 shorter events, 6.5 us)
Async XLA Ops:
  7.2 46.3 %copy-start.12 = (bf16[1,128,128]{2,1,0:T(8,128)(2,1)S(1)}, bf16[1,128,128]{2,1,0:T(8,128)(2,1)}, u32[]{:S(2)}) copy-start(bf16[1,128,128]{2,1,0:T(8,128)(2,1)} %param.8) | copy-start | bytes 98308
  7.2 122.5 %reduce-scatter.4.cloned.1.call-start = ((), (), s32[]{:S(2)}) async-start(), calls=%async_computation.1 | async-start | bytes 1114112
  7.9 48.5 %copy-start.14 = (pred[512]{0:T(512)(128)(4,1)}, pred[512]{0:T(512)(128)(4,1)S(1)}, u32[]{:S(2)}) copy-start(pred[512]{0:T(512)(128)(4,1)S(1)} %get-tuple-element.33) | copy-start | bytes 1540
  7.9 50.1 %copy-start.15 = (pred[512]{0:T(512)(128)(4,1)}, pred[512]{0:T(512)(128)(4,1)S(1)}, u32[]{:S(2)}) copy-start(pred[512]{0:T(512)(128)(4,1)S(1)} %get-tuple-element.32) | copy-start | bytes 1540
  32.0 22.6 %copy-start.8 = (bf16[1024,128]{1,0:T(8,128)(2,1)}, bf16[1024,128]{1,0:T(8,128)(2,1)S(1)}, u32[]{:S(2)}) copy-start(bf16[1024,128]{1,0:T(8,128)(2,1)S(1)} %all_gather.6) | copy-start | bytes 786436
  51.1 6.3 %copy-start.10 = (bf16[1024,128]{1,0:T(8,128)(2,1)}, bf16[1024,128]{1,0:T(8,128)(2,1)S(1)}, u32[]{:S(2)}) copy-start(bf16[1024,128]{1,0:T(8,128)(2,1)S(1)} %all_gather.7) | copy-start | bytes 786436
  52.3 2.0 %copy-start.5 = (bf16[512,128]{1,0:T(8,128)(2,1)}, bf16[512,128]{1,0:T(8,128)(2,1)S(1)}, u32[]{:S(2)}) copy-start(bf16[512,128]{1,0:T(8,128)(2,1)S(1)} %reshape_squeeze.13) | copy-start | bytes 393220
  54.3 6.4 %copy-start = (f32[512,1152]{0,1:T(8,128)}, f32[512,1152]{0,1:T(8,128)S(1)}, u32[]{:S(2)}) copy-start(f32[512,1152]{0,1:T(8,128)S(1)} %get-tuple-element.25) | copy-start | bytes 7077892
  55.8 0.8 copy-start.11
  58.6 0.8 copy-start.4
  60.1 1.2 copy-start.1
  60.6 0.9 copy-start.6
  62.0 0.8 copy-start.3
  73.2 4.2 %copy-start.2 = (bf16[512,1152]{0,1:T(8,128)(2,1)S(1)}, bf16[512,1152]{0,1:T(8,128)(2,1)}, u32[]{:S(2)}) copy-start(bf16[512,1152]{0,1:T(8,128)(2,1)} %copy-done.1) | copy-start | bytes 3538948
  73.2 4.2 %copy-start.9 = (bf16[1024,128]{1,0:T(8,128)(2,1)S(1)}, bf16[1024,128]{1,0:T(8,128)(2,1)}, u32[]{:S(2)}) copy-start(bf16[1024,128]{1,0:T(8,128)(2,1)} %copy-done.8) | copy-start | bytes 786436
  73.2 4.2 %copy-start.13 = (bf16[1,128,128]{2,1,0:T(8,128)(2,1)S(1)}, bf16[1,128,128]{2,1,0:T(8,128)(2,1)}, u32[]{:S(2)}) copy-start(bf16[1,128,128]{2,1,0:T(8,128)(2,1)} %param.8) | copy-start | bytes 98308
  73.2 6.4 %copy-start.7 = (bf16[64,1024]{1,0:T(8,128)(2,1)S(1)}, bf16[64,1024]{1,0:T(8,128)(2,1)}, u32[]{:S(2)}) copy-start(bf16[64,1024]{1,0:T(8,128)(2,1)} %reshape.88) | copy-start | bytes 393220
Sparse Core Ops, SparseCore 0:
  66.7 62.9 reduce-scatter.3
where the time goes:
time: 140 us; the launch traced here: 138 us
  waiting for transfers between devices  48.6 us (35%)
  blocking collectives  43.1 us (31%)
  between operations  15 us (11%)
  local copies, waits for them, and re-layouts  14.3 us (10%)
  matrix products  12.2 us (9%)
  other arithmetic  4.69 us (3%)
    unnamed x2, waiting for transfers between devices  48.6 us
    all_gather x1, blocking collectives, on_device(): lax.all_gather(prefix_keys, 'roll', axis=0, tiled=True)  24.1 us
    all_gather x1, blocking collectives, on_device(): lax.all_gather(prefix_values, 'roll', axis=0, tiled=True)  19 us
    unnamed x35, local copies, waits for them, and re-layouts  5.95 us
    dot_general x2, matrix products, on_device(): outputs = jnp.dot(rounded, value_rows, preferred_element_type=jnp.float32)  5.06 us
    dot_general x4, matrix products, contract_last(): lax.dot_general(left, right, (((1,), (1,)), ((), ())), preferred_element_...  2.93 us
  transfers between devices with their start and end apart: 1, of which 1 were waited for; matrix products, arithmetic and copies ran while one was open for 10% of the time, Pallas kernels for 0%

commit v1 on v0

v1 whole, which is shorter than its diff:
```python
import functools
import math

import jax
import jax.numpy as jnp
from jax import lax
from jax.experimental import pallas as pl
from jax.experimental.pallas import tpu as pltpu
from jax.sharding import PartitionSpec as P

masked_score = -1e30


def contract(left, right, dims):
    return lax.dot_general(
        left, right, ((dims[:1], dims[1:]), ((), ())), preferred_element_type=jnp.float32
    )


def spread_kernel(key_ref, value_ref, out_ref):
    head_size = key_ref.shape[1]
    for place in range(out_ref.shape[0]):
        out_ref[place, :, :head_size] = key_ref[...]
        out_ref[place, :, head_size:] = value_ref[...]


def total_kernel(pieces_ref, key_ref, value_ref):
    head_size = key_ref.shape[1]
    total = pieces_ref[0].astype(jnp.float32)
    for place in range(1, pieces_ref.shape[0]):
        total = total + pieces_ref[place].astype(jnp.float32)
    key_ref[...] = total[:, :head_size]
    value_ref[...] = total[:, head_size:]


def attention_kernel(
    length_ref,
    core_ref,
    query_ref,
    grad_ref,
    near_ref,
    far_ref,
    resp_key_ref,
    resp_value_ref,
    attended_ref,
    query_grad_ref,
    key_grad_ref,
    value_grad_ref,
    share_ref,
    key_rows,
    value_rows,
    key_sum,
    value_sum,
):
    tokens, head_size = resp_key_ref.shape
    half = near_ref.shape[0]
    prompt = 2 * half
    heads = query_ref.shape[1] // head_size
    factor = 1.0 / math.sqrt(head_size)
    exponent_factor = factor * math.log2(math.e)
    length = length_ref[0]

    for place, part_ref in enumerate((near_ref, far_ref)):
        span = slice(place * half, (place + 1) * half)
        key_rows[span] = part_ref[:, :head_size]
        value_rows[span, :head_size] = part_ref[:, head_size:]
    key_rows[prompt:] = resp_key_ref[...]
    value_rows[prompt:, :head_size] = resp_value_ref[...]
    value_rows[:, head_size:] = jnp.ones((prompt + tokens, head_size), jnp.bfloat16)

    pair = 2
    rows = pair * tokens
    token = lax.broadcasted_iota(jnp.int32, (rows, tokens), 0) % tokens
    slot = lax.broadcasted_iota(jnp.int32, (rows, tokens), 1)
    allowed = (slot <= token) & (slot < length)
    living = token < length

    for first in range(0, heads, pair):
        spans = [slice(h * head_size, (h + 1) * head_size) for h in range(first, first + pair)]
        query = jnp.concatenate([query_ref[:, span] for span in spans], axis=0)
        grad = jnp.concatenate([grad_ref[:, span] for span in spans], axis=0)
        scores = contract(query, key_rows[...], (1, 1))
        own = jnp.where(allowed, scores[:, prompt:], masked_score)
        scores = jnp.concatenate([scores[:, :prompt], own], axis=1)
        row_max = jnp.max(scores, axis=1, keepdims=True)
        weights = jnp.exp2((scores - row_max) * exponent_factor).astype(jnp.bfloat16)
        sums = contract(weights, value_rows[...], (1, 0))
        inverse = 1.0 / sums[:, head_size:]
        outputs = sums[:, :head_size] * inverse
        attended = jnp.where(living, outputs, 0.0).astype(jnp.bfloat16)
        grad = jnp.where(living, grad.astype(jnp.float32) * inverse, 0.0).astype(jnp.bfloat16)
        correction = jnp.sum(grad.astype(jnp.float32) * outputs, axis=1, keepdims=True)
        grad_weights = contract(grad, value_rows[:, :head_size], (1, 1))
        grad_scores = (weights.astype(jnp.float32) * (grad_weights - correction)).astype(jnp.bfloat16)
        query_grad = (contract(grad_scores, key_rows[...], (1, 0)) * factor).astype(jnp.bfloat16)
        for place, span in enumerate(spans):
            part = slice(place * tokens, (place + 1) * tokens)
            attended_ref[:, span] = attended[part]
            query_grad_ref[:, span] = query_grad[part]
        key_part = contract(query, grad_scores, (0, 0))
        value_part = contract(grad, weights, (0, 0))
        if first == 0:
            key_sum[...] = key_part
            value_sum[...] = value_part
        else:
            key_sum[...] += key_part
            value_sum[...] += value_part

    key_total = (key_sum[...] * factor).astype(jnp.bfloat16).T
    value_total = value_sum[...].astype(jnp.bfloat16).T
    key_grad_ref[...] = key_total[prompt:]
    value_grad_ref[...] = value_total[prompt:]
    owned = share_ref.shape[1]
    core = core_ref[0]
    for place in range(prompt // owned):
        side, chip = divmod(place, half // owned)
        rank = 2 * chip + (core if side == 0 else 1 - core)
        span = slice(place * owned, (place + 1) * owned)
        share_ref[rank, :, :head_size] = key_total[span]
        share_ref[rank, :, head_size:] = value_total[span]


def attention(length, core, queries, grads, near, far, resp_keys, resp_values, owned):
    tokens, head_size = resp_keys.shape
    prompt = 2 * near.shape[0]
    key_count = prompt + tokens
    vmem = pl.BlockSpec(memory_space=pltpu.VMEM)
    return pl.pallas_call(
        attention_kernel,
        out_shape=(
            jax.ShapeDtypeStruct(queries.shape, jnp.bfloat16),
            jax.ShapeDtypeStruct(queries.shape, jnp.bfloat16),
            jax.ShapeDtypeStruct(resp_keys.shape, jnp.bfloat16),
            jax.ShapeDtypeStruct(resp_keys.shape, jnp.bfloat16),
            jax.ShapeDtypeStruct((prompt // owned, owned, 2 * head_size), jnp.bfloat16),
        ),
        in_specs=[pl.BlockSpec(memory_space=pltpu.SMEM)] * 2 + [vmem] * 6,
        out_specs=[vmem] * 5,
        scratch_shapes=[
            pltpu.VMEM((key_count, head_size), jnp.bfloat16),
            pltpu.VMEM((key_count, 2 * head_size), jnp.bfloat16),
            pltpu.VMEM((head_size, key_count), jnp.float32),
            pltpu.VMEM((head_size, key_count), jnp.float32),
        ],
        compiler_params=pltpu.CompilerParams(vmem_limit_bytes=48 * 1024 * 1024),
    )(length, core, queries, grads, near, far, resp_keys, resp_values)


def on_device(ranks, queries, resp_keys, resp_values, prefix_keys, prefix_values, grad_out, lengths):
    head_size = resp_keys.shape[2]
    owned = prefix_keys.shape[0]
    chips = ranks // 2
    vmem = pl.BlockSpec(memory_space=pltpu.VMEM)
    sent = pl.pallas_call(
        spread_kernel,
        out_shape=jax.ShapeDtypeStruct((chips, owned, 2 * head_size), jnp.bfloat16),
        in_specs=[vmem] * 2,
        out_specs=vmem,
    )(prefix_keys, prefix_values)
    same_core = [list(range(core, ranks, 2)) for core in range(2)]
    near = lax.all_to_all(sent, "roll", 0, 0, axis_index_groups=same_core)
    near = near.reshape(chips * owned, 2 * head_size)
    far = lax.ppermute(near, "roll", [(rank, rank ^ 1) for rank in range(ranks)])
    core = (lax.axis_index("roll") % 2).astype(jnp.int32)[None]
    attended, query_grad, key_grad, value_grad, share = attention(
        lengths, core, queries[0], grad_out[0], near, far, resp_keys[0], resp_values[0], owned
    )
    pieces = lax.all_to_all(share, "roll", 0, 0)
    key_total, value_total = pl.pallas_call(
        total_kernel,
        out_shape=(jax.ShapeDtypeStruct((owned, head_size), jnp.float32),) * 2,
        in_specs=[vmem],
        out_specs=[vmem] * 2,
    )(pieces)
    return (
        attended[None],
        query_grad[None],
        key_grad[None],
        value_grad[None],
        key_total,
        value_total,
    )


def solution(mesh):
    rolls = P(("prompt", "roll"), None, "head")
    prompts = P(("prompt", "roll"), "head")
    return jax.shard_map(
        functools.partial(on_device, mesh.shape["roll"]),
        mesh=mesh,
        in_specs=(rolls, rolls, rolls, prompts, prompts, rolls, P(("prompt", "roll"))),
        out_specs=(rolls, rolls, rolls, rolls, prompts, prompts),
        check_vma=False,
    )
```

time: 140 us -> 44.9 us (0.32); the launches traced: 138 us -> 44.5 us
  waiting for transfers between devices: 48.6 us -> 0.48 us
  blocking collectives: 43.1 us -> 26.3 us
  local copies, waits for them, and re-layouts: 14.3 us -> 0.02 us
  between operations: 15 us -> 1.31 us
  matrix products: 12.2 us -> 0 us
  Pallas kernels: 0 us -> 9.68 us
  starting transfers between devices: 0.04 us -> 6.72 us
  other arithmetic: 4.69 us -> 0 us
    unnamed x2 -> x0, waiting for transfers between devices: 48.6 us -> none
    all_gather x2 -> x0, blocking collectives: 43.1 us -> none  [the longest x1 24.1 us: on_device(): lax.all_gather(prefix_keys, 'roll', axis=0, tiled=True)]
    all_to_all x0 -> x2, blocking collectives: none -> 26.3 us  [the longest x1 13.3 us: on_device(): pieces = lax.all_to_all(share, 'roll', 0, 0)]
    dot_general x12 -> x0, matrix products: 12.2 us -> none  [the longest x2 5.06 us: on_device(): outputs = jnp.dot(rounded, value_rows, preferred_element_type=jnp.float32)]
    pallas_call x0 -> x3, Pallas kernels: none -> 9.68 us  [the longest x1 6.47 us: attention(): pl.pallas_call(attention_kernel, out_shape=(jax.ShapeDtypeStruct(queries....]
    ppermute x0 -> x1, starting transfers between devices: none -> 6.72 us  [on_device(): lax.ppermute(near, 'roll', [(rank, rank ^ 1) for rank in range(ranks)])]
    unnamed x35 -> x8, local copies, waits for them, and re-layouts: 5.95 us -> 0.02 us
    slice x5 -> x0, local copies, waits for them, and re-layouts: 3.6 us -> none  [the longest x1 1.4 us: on_device(): shares[:, head_size:]]
  transfers between devices with their start and end apart: 1 -> 1, of which waited for: 1 -> 1; matrix products, arithmetic and copies ran while one was open for 10% -> 0% of each run, Pallas kernels for 0% -> 0%
where the time goes in v1:
time: 44.9 us; the launch traced here: 44.5 us
  blocking collectives  26.3 us (59%)
  Pallas kernels  9.68 us (22%)
  starting transfers between devices  6.72 us (15%)
  between operations  1.31 us (3%)
  waiting for transfers between devices  0.48 us (1%)
    all_to_all x1, blocking collectives, on_device(): pieces = lax.all_to_all(share, 'roll', 0, 0)  13.3 us
    all_to_all x1, blocking collectives, on_device(): near = lax.all_to_all(sent, 'roll', 0, 0, axis_index_groups=same_core)  12.9 us
    ppermute x1, starting transfers between devices, on_device(): lax.ppermute(near, 'roll', [(rank, rank ^ 1) for rank in range(ranks)])  6.72 us
    pallas_call x1, Pallas kernels, attention(): pl.pallas_call(attention_kernel, out_shape=(jax.ShapeDtypeStruct(queries....  6.47 us
    pallas_call x1, Pallas kernels, on_device(): pl.pallas_call(total_kernel, out_shape=(jax.ShapeDtypeStruct((owned, head...  1.73 us
    pallas_call x1, Pallas kernels, on_device(): pl.pallas_call(spread_kernel, out_shape=jax.ShapeDtypeStruct((chips, owne...  1.48 us
  transfers between devices with their start and end apart: 1, of which 1 were waited for; matrix products, arithmetic and copies ran while one was open for 0% of the time, Pallas kernels for 0%

profile of v1, /device:TPU:1, one launch (start us, length us, event | category | flops | bytes accessed | tf_op | source)
XLA Modules:
  0.0 44.5 jit_solution(7702465219759610203)
XLA Ops:
  0.6 0.0 copy-start.3
  0.6 1.5 %shard_map.118 = bf16[8,64,256]{2,1,0:T(8,128)(2,1)} custom-call(bf16[64,128]{1,0:T(8,128)(2,1)} %key_ref.1, bf16[64,128]{1,0:T(8,128)(2,1)} %value_ref.1), custom_call_target="tpu_custom_call" | custom-call | tf_op jit(solution)/shard_map/pallas_call | solution.py:154
  2.1 0.0 copy-start
  2.1 0.0 copy-start.1
  2.1 12.9 %all_to_all.10 = bf16[8,64,256]{2,1,0:T(8,128)(2,1)S(1)} all-to-all(bf16[8,64,256]{2,1,0:T(8,128)(2,1)} %shard_map.118), channel_id=1, replica_groups={{0,8,16,24,32,40,48,56},{4,12,20,28,36,44,52,60},{1,9,17,25,33,41,49,57..., dimensions={0} | all-to-all | bytes 524288 | tf_op jit(solution)/shard_map/all_to_all | solution.py:161
  15.0 0.0 copy-start.2
  15.0 6.7 %collective-permute-start = (bf16[512,256]{1,0:T(8,128)(2,1)S(1)}, bf16[512,256]{1,0:T(8,128)(2,1)S(1)}, u32[]{:S(2)}, u32[]{:S(2)}) collective-permute-start(bf16[512,256]{1,0:T(8,128)(2,1)S(1)} %bitcast.10), channel_id=1, source_target_pairs={{0,4},{4,0},{8,12},{12,8},{16,20},{20,16},{24,28},{28,24},{32,36},... | collective-permute-start | bytes 786440 | tf_op jit(solution)/shard_map/ppermute | solution.py:163
  22.4 0.5 %collective-permute-done.far_ref = bf16[512,256]{1,0:T(8,128)(2,1)S(1)} collective-permute-done((bf16[512,256]{1,0:T(8,128)(2,1)S(1)}, bf16[512,256]{1,0:T(8,128)(2,1)S(1)}, u32[]{:S(2)}, u32[]{:S(2)}) %collective-permute-start) | collective-permute-done | bytes 262176 | tf_op jit(solution)/shard_map/ppermute | solution.py:163
  22.9 0.0 copy-done.3
  22.9 0.0 copy-done
  22.9 0.0 copy-done.1
  22.9 0.0 copy-done.2
  22.9 6.5 %shard_map.119 = (bf16[128,1024]{1,0:T(8,128)(2,1)}, bf16[128,1024]{1,0:T(8,128)(2,1)}, bf16[128,128]{1,0:T(8,128)(2,1)}, bf16[128,128]{1,0:T(8,128)(2,1)}, bf16[16,64,256]{2,1,0:T(8,128)(2,1)S(1)}) custom-call(s32[1]{0:T(128)S(6)} %copy.13.length_ref, s32[1]{0:T(128)} %bitcast.core_ref, bf16[128,1024]{1,0:T(8,128)(2,1)S(1)} %bitcast.12, ...), custom_call_target="tpu_custom_call" | custom-call | tf_op jit(solution)/shard_map/pallas_call | solution.py:128
  29.4 13.3 %all_to_all.11.pieces_ref = bf16[16,64,256]{2,1,0:T(8,128)(2,1)} all-to-all(bf16[16,64,256]{2,1,0:T(8,128)(2,1)S(1)} %get-tuple-element.17), channel_id=1, replica_groups=mesh['prompt'=8,'roll'=16,'head'=4] {'roll'}, dimensions={0} | all-to-all | bytes 1048576 | tf_op jit(solution)/shard_map/all_to_all | solution.py:168
  42.7 1.7 %shard_map.120 = (f32[64,128]{1,0:T(8,128)}, f32[64,128]{1,0:T(8,128)}) custom-call(bf16[16,64,256]{2,1,0:T(8,128)(2,1)} %all_to_all.11.pieces_ref), custom_call_target="tpu_custom_call" | custom-call | tf_op jit(solution)/shard_map/pallas_call | solution.py:169
Async XLA Ops:
  0.6 22.3 %copy-start.3 = (bf16[1,128,128]{2,1,0:T(8,128)(2,1)S(1)}, bf16[1,128,128]{2,1,0:T(8,128)(2,1)}, u32[]{:S(2)}) copy-start(bf16[1,128,128]{2,1,0:T(8,128)(2,1)} %param.9) | copy-start | bytes 98308
  2.1 20.8 %copy-start = (bf16[1,128,1024]{2,1,0:T(8,128)(2,1)S(1)}, bf16[1,128,1024]{2,1,0:T(8,128)(2,1)}, u32[]{:S(2)}) copy-start(bf16[1,128,1024]{2,1,0:T(8,128)(2,1)} %param.7) | copy-start | bytes 786436
  2.1 20.8 %copy-start.1 = (bf16[1,128,1024]{2,1,0:T(8,128)(2,1)S(1)}, bf16[1,128,1024]{2,1,0:T(8,128)(2,1)}, u32[]{:S(2)}) copy-start(bf16[1,128,1024]{2,1,0:T(8,128)(2,1)} %param.12) | copy-start | bytes 786436
  15.0 7.9 %copy-start.2 = (bf16[1,128,128]{2,1,0:T(8,128)(2,1)S(1)}, bf16[1,128,128]{2,1,0:T(8,128)(2,1)}, u32[]{:S(2)}) copy-start(bf16[1,128,128]{2,1,0:T(8,128)(2,1)} %param.8) | copy-start | bytes 98308
  15.0 7.9 %collective-permute-start = (bf16[512,256]{1,0:T(8,128)(2,1)S(1)}, bf16[512,256]{1,0:T(8,128)(2,1)S(1)}, u32[]{:S(2)}, u32[]{:S(2)}) collective-permute-start(bf16[512,256]{1,0:T(8,128)(2,1)S(1)} %bitcast.10), channel_id=1, source_target_pairs={{0,4},{4,0},{8,12},{12,8},{16,20},{20,16},{24,28},{28,24},{32,36},... | collective-permute-start | bytes 786440 | tf_op jit(solution)/shard_map/ppermute | solution.py:163

commit v2 on v1

v2 whole, which is shorter than its diff:
```python
import functools
import math

import jax
import jax.numpy as jnp
from jax import lax
from jax.experimental import pallas as pl
from jax.experimental.pallas import tpu as pltpu
from jax.sharding import PartitionSpec as P

masked_score = -1e30


def contract(left, right, dims):
    return lax.dot_general(
        left, right, ((dims[:1], dims[1:]), ((), ())), preferred_element_type=jnp.float32
    )


def attention_kernel(
    length_ref,
    query_ref,
    grad_ref,
    prefix_ref,
    resp_key_ref,
    resp_value_ref,
    attended_ref,
    query_grad_ref,
    key_grad_ref,
    value_grad_ref,
    share_ref,
    key_rows,
    value_rows,
    key_sum,
    value_sum,
):
    tokens, head_size = resp_key_ref.shape
    ranks, owned, _ = prefix_ref.shape
    prompt = ranks * owned
    heads = query_ref.shape[1] // head_size
    factor = 1.0 / math.sqrt(head_size)
    exponent_factor = factor * math.log2(math.e)
    length = length_ref[0]

    for rank in range(ranks):
        span = slice(rank * owned, (rank + 1) * owned)
        key_rows[span] = prefix_ref[rank, :, :head_size]
        value_rows[span, :head_size] = prefix_ref[rank, :, head_size:]
    key_rows[prompt:] = resp_key_ref[...]
    value_rows[prompt:, :head_size] = resp_value_ref[...]
    value_rows[:, head_size:] = jnp.ones((prompt + tokens, head_size), jnp.bfloat16)
    key_sum[...] = jnp.zeros_like(key_sum)
    value_sum[...] = jnp.zeros_like(value_sum)

    pair = 2
    rows = pair * tokens
    token = lax.broadcasted_iota(jnp.int32, (rows, tokens), 0) % tokens
    slot = lax.broadcasted_iota(jnp.int32, (rows, tokens), 1)
    allowed = (slot <= token) & (slot < length)
    living = token < length

    @pl.loop(0, heads, step=pair)
    def _(first):
        spans = [
            pl.ds(pl.multiple_of((first + place) * head_size, head_size), head_size)
            for place in range(pair)
        ]
        query = jnp.concatenate([query_ref[:, span] for span in spans], axis=0)
        grad = jnp.concatenate([grad_ref[:, span] for span in spans], axis=0)
        scores = contract(query, key_rows[...], (1, 1))
        own = jnp.where(allowed, scores[:, prompt:], masked_score)
        scores = jnp.concatenate([scores[:, :prompt], own], axis=1)
        row_max = jnp.max(scores, axis=1, keepdims=True)
        weights = jnp.exp2((scores - row_max) * exponent_factor).astype(jnp.bfloat16)
        sums = contract(weights, value_rows[...], (1, 0))
        inverse = 1.0 / sums[:, head_size:]
        outputs = sums[:, :head_size] * inverse
        attended = jnp.where(living, outputs, 0.0).astype(jnp.bfloat16)
        grad = jnp.where(living, grad.astype(jnp.float32) * inverse, 0.0).astype(jnp.bfloat16)
        correction = jnp.sum(grad.astype(jnp.float32) * outputs, axis=1, keepdims=True)
        grad_weights = contract(grad, value_rows[:, :head_size], (1, 1))
        grad_scores = (weights.astype(jnp.float32) * (grad_weights - correction)).astype(jnp.bfloat16)
        query_grad = (contract(grad_scores, key_rows[...], (1, 0)) * factor).astype(jnp.bfloat16)
        for place, span in enumerate(spans):
            part = slice(place * tokens, (place + 1) * tokens)
            attended_ref[:, span] = attended[part]
            query_grad_ref[:, span] = query_grad[part]
        key_sum[...] += contract(query, grad_scores, (0, 0))
        value_sum[...] += contract(grad, weights, (0, 0))

    key_total = (key_sum[...] * factor).astype(jnp.bfloat16).T
    value_total = value_sum[...].astype(jnp.bfloat16).T
    key_grad_ref[...] = key_total[prompt:]
    value_grad_ref[...] = value_total[prompt:]
    for rank in range(ranks):
        span = slice(rank * owned, (rank + 1) * owned)
        share_ref[rank, :, :head_size] = key_total[span]
        share_ref[rank, :, head_size:] = value_total[span]


def attention(length, queries, grads, prefix, resp_keys, resp_values):
    tokens, head_size = resp_keys.shape
    key_count = prefix.shape[0] * prefix.shape[1] + tokens
    vmem = pl.BlockSpec(memory_space=pltpu.VMEM)
    return pl.pallas_call(
        attention_kernel,
        out_shape=(
            jax.ShapeDtypeStruct(queries.shape, jnp.bfloat16),
            jax.ShapeDtypeStruct(queries.shape, jnp.bfloat16),
            jax.ShapeDtypeStruct(resp_keys.shape, jnp.bfloat16),
            jax.ShapeDtypeStruct(resp_keys.shape, jnp.bfloat16),
            jax.ShapeDtypeStruct(prefix.shape, jnp.bfloat16),
        ),
        in_specs=[pl.BlockSpec(memory_space=pltpu.SMEM)] + [vmem] * 5,
        out_specs=[vmem] * 5,
        scratch_shapes=[
            pltpu.VMEM((key_count, head_size), jnp.bfloat16),
            pltpu.VMEM((key_count, 2 * head_size), jnp.bfloat16),
            pltpu.VMEM((head_size, key_count), jnp.float32),
            pltpu.VMEM((head_size, key_count), jnp.float32),
        ],
        compiler_params=pltpu.CompilerParams(vmem_limit_bytes=48 * 1024 * 1024),
    )(length, queries, grads, prefix, resp_keys, resp_values)


def on_device(ranks, queries, resp_keys, resp_values, prefix_keys, prefix_values, grad_out, lengths):
    head_size = resp_keys.shape[2]
    own = jnp.concatenate([prefix_keys, prefix_values], axis=1)
    sent = jnp.broadcast_to(own[None], (ranks, *own.shape))
    prefix = lax.all_to_all(sent, "roll", 0, 0)
    attended, query_grad, key_grad, value_grad, share = attention(
        lengths, queries[0], grad_out[0], prefix, resp_keys[0], resp_values[0]
    )
    pieces = lax.all_to_all(share, "roll", 0, 0)
    total = pieces[0].astype(jnp.float32)
    for rank in range(1, ranks):
        total = total + pieces[rank].astype(jnp.float32)
    return (
        attended[None],
        query_grad[None],
        key_grad[None],
        value_grad[None],
        total[:, :head_size],
        total[:, head_size:],
    )


def solution(mesh):
    rolls = P(("prompt", "roll"), None, "head")
    prompts = P(("prompt", "roll"), "head")
    return jax.shard_map(
        functools.partial(on_device, mesh.shape["roll"]),
        mesh=mesh,
        in_specs=(rolls, rolls, rolls, prompts, prompts, rolls, P(("prompt", "roll"))),
        out_specs=(rolls, rolls, rolls, rolls, prompts, prompts),
        check_vma=False,
    )
```

time: 44.9 us -> 44.4 us (0.989)
  blocking collectives: 26.3 us -> 13.5 us
  waiting for transfers between devices: 0.48 us -> 9.23 us
  starting transfers between devices: 6.72 us -> 10.4 us
  Pallas kernels: 9.68 us -> 7.27 us
  local copies, waits for them, and re-layouts: 0.02 us -> 1.49 us
  other arithmetic: 0 us -> 0.82 us
    all_to_all x1 -> x0, blocking collectives: 12.9 us -> none  [on_device(): near = lax.all_to_all(sent, 'roll', 0, 0, axis_index_groups=same_core)]
    all_to_all x0 -> x1, starting transfers between devices: none -> 10.4 us  [on_device(): prefix = lax.all_to_all(sent, 'roll', 0, 0)]
    all_to_all x0 -> x1, waiting for transfers between devices: none -> 9.23 us  [on_device(): prefix = lax.all_to_all(sent, 'roll', 0, 0)]
    ppermute x1 -> x0, starting transfers between devices: 6.72 us -> none  [on_device(): lax.ppermute(near, 'roll', [(rank, rank ^ 1) for rank in range(ranks)])]
    pallas_call x2 -> x0, Pallas kernels: 3.21 us -> none  [the longest x1 1.73 us: on_device(): pl.pallas_call(total_kernel, out_shape=(jax.ShapeDtypeStruct((owned, head...]
    broadcast_in_dim x0 -> x1, local copies, waits for them, and re-layouts: none -> 0.84 us  [on_device(): sent = jnp.broadcast_to(own[None], (ranks, *own.shape))]
    pallas_call x1, Pallas kernels: 6.47 us -> 7.27 us  [attention(): pl.pallas_call(attention_kernel, out_shape=(jax.ShapeDtypeStruct(queries....]
    concatenate x0 -> x1, other arithmetic: none -> 0.74 us  [on_device(): own = jnp.concatenate([prefix_keys, prefix_values], axis=1)]
where the time goes in v2:
time: 44.4 us; the launch traced here: 44 us
  blocking collectives  13.5 us (30%)
  starting transfers between devices  10.4 us (23%)
  waiting for transfers between devices  9.23 us (21%)
  Pallas kernels  7.27 us (16%)
  local copies, waits for them, and re-layouts  1.49 us (3%)
  between operations  1.31 us (3%)
  other arithmetic  0.82 us (2%)
    all_to_all x1, blocking collectives, on_device(): pieces = lax.all_to_all(share, 'roll', 0, 0)  13.5 us
    all_to_all x1, starting transfers between devices, on_device(): prefix = lax.all_to_all(sent, 'roll', 0, 0)  10.4 us
    all_to_all x1, waiting for transfers between devices, on_device(): prefix = lax.all_to_all(sent, 'roll', 0, 0)  9.23 us
    pallas_call x1, Pallas kernels, attention(): pl.pallas_call(attention_kernel, out_shape=(jax.ShapeDtypeStruct(queries....  7.27 us
  transfers between devices with their start and end apart: 1, of which 1 were waited for; matrix products, arithmetic and copies ran while one was open for 0% of the time, Pallas kernels for 0%

profile of v2, /device:TPU:1, one launch (start us, length us, event | category | flops | bytes accessed | tf_op | source)
XLA Modules:
  0.0 44.0 jit_solution(18399822858268890890)
XLA Ops:
  0.6 0.7 %pad_maximum_fusion = bf16[64,256]{1,0:T(8,128)(2,1)S(1)} fusion(bf16[64,128]{1,0:T(8,128)(2,1)} %param.11, bf16[64,128]{1,0:T(8,128)(2,1)} %param.10), kind=kLoop, calls=%fused_computation.2 | loop fusion | flops 65536 | bytes 65536 | tf_op jit(solution)/shard_map/concatenate | solution.py:128
  1.4 0.8 %broadcast_in_dim.18 = bf16[16,64,256]{2,1,0:T(8,128)(2,1)} broadcast(bf16[64,256]{1,0:T(8,128)(2,1)S(1)} %pad_maximum_fusion), dimensions={1,2} | broadcast | bytes 557056 | tf_op jit(solution)/shard_map/broadcast_in_dim | solution.py:129
  2.2 0.0 copy-start
  2.2 0.0 copy-start.1
  2.2 0.0 copy-start.2
  2.2 0.0 copy-start.3
  2.2 10.4 %all-to-all-start = ((bf16[16,64,256]{2,1,0:T(8,128)(2,1)}), bf16[16,64,256]{2,1,0:T(8,128)(2,1)S(1)}, u32[]{:S(2)}, u32[]{:S(2)}) async-start(bf16[16,64,256]{2,1,0:T(8,128)(2,1)} %broadcast_in_dim.18), calls=%async_computation | async-start | bytes 1048576 | tf_op jit(solution)/shard_map/all_to_all | solution.py:130
  13.3 9.2 %all-to-all-done.prefix_ref = bf16[16,64,256]{2,1,0:T(8,128)(2,1)S(1)} async-done(((bf16[16,64,256]{2,1,0:T(8,128)(2,1)}), bf16[16,64,256]{2,1,0:T(8,128)(2,1)S(1)}, u32[]{:S(2)}, u32[]{:S(2)}) %all-to-all-start) | async-done | bytes 524320 | tf_op jit(solution)/shard_map/all_to_all | solution.py:130
  22.5 0.0 copy-done
  22.5 0.0 copy-done.1
  22.5 0.0 copy-done.2
  22.5 0.0 copy-done.3
  22.5 7.3 %shard_map.118 = (bf16[128,1024]{1,0:T(8,128)(2,1)}, bf16[128,1024]{1,0:T(8,128)(2,1)}, bf16[128,128]{1,0:T(8,128)(2,1)}, bf16[128,128]{1,0:T(8,128)(2,1)}, bf16[16,64,256]{2,1,0:T(8,128)(2,1)S(1)}) custom-call(s32[1]{0:T(128)S(6)} %copy.13.length_ref, bf16[128,1024]{1,0:T(8,128)(2,1)S(1)} %bitcast.15, bf16[128,1024]{1,0:T(8,128)(2,1)S(1)} %bitcast.16, ...), custom_call_target="tpu_custom_call" | custom-call | tf_op jit(solution)/shard_map/pallas_call | solution.py:105
  29.8 13.5 %all_to_all.10 = bf16[16,64,256]{2,1,0:T(8,128)(2,1)S(1)} all-to-all(bf16[16,64,256]{2,1,0:T(8,128)(2,1)S(1)} %get-tuple-element.15), channel_id=1, replica_groups=mesh['prompt'=8,'roll'=16,'head'=4] {'roll'}, dimensions={0} | all-to-all | bytes 1048576 | tf_op jit(solution)/shard_map/all_to_all | solution.py:134
  43.3 0.1 convert_add_fusion
  43.4 0.6 %fusion = (f32[64,128]{1,0:T(8,128)}, f32[64,128]{1,0:T(8,128)}) fusion(f32[64,256]{1,0:T(8,128)S(1)} %convert_add_fusion), kind=kLoop, calls=%fused_computation.3 | loop fusion | bytes 131072 | tf_op jit(solution)/shard_map/slice | solution.py:144
Async XLA Ops:
  2.2 20.3 %copy-start = (bf16[1,128,1024]{2,1,0:T(8,128)(2,1)S(1)}, bf16[1,128,1024]{2,1,0:T(8,128)(2,1)}, u32[]{:S(2)}) copy-start(bf16[1,128,1024]{2,1,0:T(8,128)(2,1)} %param.7) | copy-start | bytes 786436
  2.2 20.3 %copy-start.1 = (bf16[1,128,1024]{2,1,0:T(8,128)(2,1)S(1)}, bf16[1,128,1024]{2,1,0:T(8,128)(2,1)}, u32[]{:S(2)}) copy-start(bf16[1,128,1024]{2,1,0:T(8,128)(2,1)} %param.12) | copy-start | bytes 786436
  2.2 20.3 %copy-start.2 = (bf16[1,128,128]{2,1,0:T(8,128)(2,1)S(1)}, bf16[1,128,128]{2,1,0:T(8,128)(2,1)}, u32[]{:S(2)}) copy-start(bf16[1,128,128]{2,1,0:T(8,128)(2,1)} %param.8) | copy-start | bytes 98308
  2.2 20.3 %copy-start.3 = (bf16[1,128,128]{2,1,0:T(8,128)(2,1)S(1)}, bf16[1,128,128]{2,1,0:T(8,128)(2,1)}, u32[]{:S(2)}) copy-start(bf16[1,128,128]{2,1,0:T(8,128)(2,1)} %param.9) | copy-start | bytes 98308
  2.2 20.3 %all-to-all-start = ((bf16[16,64,256]{2,1,0:T(8,128)(2,1)}), bf16[16,64,256]{2,1,0:T(8,128)(2,1)S(1)}, u32[]{:S(2)}, u32[]{:S(2)}) async-start(bf16[16,64,256]{2,1,0:T(8,128)(2,1)} %broadcast_in_dim.18), calls=%async_computation | async-start | bytes 1048576 | tf_op jit(solution)/shard_map/all_to_all | solution.py:130

commit v3 on v2

v3 whole, which is shorter than its diff:
```python
import functools
import math

import jax
import jax.numpy as jnp
from jax import lax
from jax.experimental import pallas as pl
from jax.experimental.pallas import tpu as pltpu
from jax.sharding import PartitionSpec as P

masked_score = -1e30
GROUP = 4


def contract(left, right, dims):
    return lax.dot_general(
        left, right, ((dims[:1], dims[1:]), ((), ())), preferred_element_type=jnp.float32
    )


def head_parts(columns, tokens, head_size):
    return [
        (slice(head * tokens, (head + 1) * tokens), slice(head * head_size, (head + 1) * head_size))
        for head in range(columns // head_size)
    ]


def spread_kernel(length_ref, key_hbm, value_hbm, out_ref, living_ref, own, sems):
    head_size = key_hbm.shape[1]
    copies = [
        pltpu.make_async_copy(source, own.at[place], sems.at[place])
        for place, source in enumerate((key_hbm, value_hbm))
    ]
    for copy in copies:
        copy.start()
    token = lax.broadcasted_iota(jnp.int32, living_ref.shape, 0)
    living_ref[...] = (token < length_ref[0]).astype(jnp.float32)
    for copy in copies:
        copy.wait()
    for place in range(out_ref.shape[0]):
        out_ref[place, :, :head_size] = own[0]
        out_ref[place, :, head_size:] = own[1]


def attention_kernel(
    living_ref,
    query_ref,
    grad_ref,
    resp_key_ref,
    resp_value_ref,
    prefix_ref,
    attended_hbm,
    query_grad_hbm,
    key_grad_hbm,
    value_grad_hbm,
    share_ref,
    key_rows,
    value_rows,
    attended_ref,
    query_grad_ref,
    own_grad_ref,
    sems,
):
    tokens, head_size = resp_key_ref.shape
    ranks, owned, _ = prefix_ref.shape
    prompt = ranks * owned
    heads = query_ref.shape[1] // head_size
    factor = 1.0 / math.sqrt(head_size)
    exponent_factor = factor * math.log2(math.e)
    parts = head_parts(query_ref.shape[1], tokens, head_size)
    copies = []

    def send(source, target):
        copy = pltpu.make_async_copy(source, target, sems.at[len(copies)])
        copy.start()
        copies.append(copy)

    for rank in range(ranks):
        span = slice(rank * owned, (rank + 1) * owned)
        key_rows[span] = prefix_ref[rank, :, :head_size]
        value_rows[span, :head_size] = prefix_ref[rank, :, head_size:]
    key_rows[prompt:] = resp_key_ref[...]
    value_rows[prompt:, :head_size] = resp_value_ref[...]
    value_rows[:, head_size:] = jnp.ones((prompt + tokens, head_size), jnp.bfloat16)

    groups = [parts[at : at + GROUP] for at in range(0, heads, GROUP)]
    stacked = [
        [jnp.concatenate([ref[:, span] for _, span in group], axis=0) for group in groups]
        for ref in (query_ref, grad_ref)
    ]
    queries, grads = stacked
    living = jnp.concatenate([living_ref[...]] * GROUP, axis=0) > 0.0
    token = lax.broadcasted_iota(jnp.int32, (GROUP * tokens, tokens), 0) % tokens
    allowed = lax.broadcasted_iota(jnp.int32, (GROUP * tokens, tokens), 1) <= token

    def exponentials(scores):
        own = jnp.where(allowed, scores[:, prompt:], masked_score)
        scores = jnp.concatenate([scores[:, :prompt], own], axis=1)
        row_max = jnp.max(scores, axis=1, keepdims=True)
        return jnp.exp2((scores - row_max) * exponent_factor).astype(jnp.bfloat16)

    def normalised(index, sums):
        inverse = 1.0 / sums[:, head_size:]
        outputs = sums[:, :head_size] * inverse
        attended = jnp.where(living, outputs, 0.0).astype(jnp.bfloat16)
        for place, (_, span) in enumerate(groups[index]):
            attended_ref[:, span] = attended[place * tokens : (place + 1) * tokens]
        grad = jnp.where(living, grads[index].astype(jnp.float32) * inverse, 0.0).astype(jnp.bfloat16)
        return grad, jnp.sum(grad.astype(jnp.float32) * outputs, axis=1, keepdims=True)

    count = len(groups)
    scores, weights, sums, states, grad_weights, grad_scores = ([None] * count for _ in range(6))
    for step in range(count + 1):
        if step < count:
            scores[step] = contract(queries[step], key_rows[...], (1, 1))
        if step > 0:
            weights[step - 1] = exponentials(scores[step - 1])
            sums[step - 1] = contract(weights[step - 1], value_rows[...], (1, 0))
    for step in range(count + 1):
        if step < count:
            states[step] = normalised(step, sums[step])
            grad_weights[step] = contract(states[step][0], value_rows[:, :head_size], (1, 1))
        if step > 0:
            last = step - 1
            shifted = (grad_weights[last] - states[last][1]).astype(jnp.bfloat16)
            grad_scores[last] = weights[last] * shifted
            query_grad = contract(grad_scores[last], key_rows[...], (1, 0)) * factor
            for place, (_, span) in enumerate(groups[last]):
                part = query_grad[place * tokens : (place + 1) * tokens]
                query_grad_ref[:, span] = part.astype(jnp.bfloat16)
    send(attended_ref, attended_hbm)
    query = jnp.concatenate(queries, axis=0)
    grad = jnp.concatenate([state[0] for state in states], axis=0)
    weights = jnp.concatenate(weights, axis=0)
    grad_scores = jnp.concatenate(grad_scores, axis=0)
    send(query_grad_ref, query_grad_hbm)
    key_total = (contract(query, grad_scores, (0, 0)) * factor).astype(jnp.bfloat16)
    value_total = contract(grad, weights, (0, 0)).astype(jnp.bfloat16)
    own_grad_ref[0] = key_total[:, prompt:].T
    send(own_grad_ref.at[0], key_grad_hbm)
    own_grad_ref[1] = value_total[:, prompt:].T
    send(own_grad_ref.at[1], value_grad_hbm)
    for place, total in enumerate((key_total, value_total)):
        turned = total[:, :prompt].T
        for rank in range(ranks):
            lanes = slice(place * head_size, (place + 1) * head_size)
            share_ref[rank, :, lanes] = turned[rank * owned : (rank + 1) * owned]
    for copy in copies:
        copy.wait()


def on_device(ranks, queries, resp_keys, resp_values, prefix_keys, prefix_values, grad_out, lengths):
    tokens, columns = queries.shape[1:]
    owned, head_size = prefix_keys.shape
    key_count = ranks * owned + tokens
    half = jnp.bfloat16
    vmem = pl.BlockSpec(memory_space=pltpu.VMEM)
    anywhere = pl.BlockSpec(memory_space=pl.ANY)

    sent, living = pl.pallas_call(
        spread_kernel,
        out_shape=(
            pltpu.VMEM((ranks, owned, 2 * head_size), half),
            pltpu.VMEM((tokens, head_size), jnp.float32),
        ),
        in_specs=[pl.BlockSpec(memory_space=pltpu.SMEM)] + [pl.BlockSpec(memory_space=pltpu.HBM)] * 2,
        out_specs=[vmem] * 2,
        scratch_shapes=[pltpu.VMEM((2, owned, head_size), half), pltpu.SemaphoreType.DMA((2,))],
    )(lengths, prefix_keys, prefix_values)
    prefix = lax.all_to_all(sent, "roll", 0, 0)
    attended, query_grad, key_grad, value_grad, share = pl.pallas_call(
        attention_kernel,
        out_shape=(
            jax.ShapeDtypeStruct((tokens, columns), half),
            jax.ShapeDtypeStruct((tokens, columns), half),
            jax.ShapeDtypeStruct((tokens, head_size), half),
            jax.ShapeDtypeStruct((tokens, head_size), half),
            pltpu.VMEM((ranks, owned, 2 * head_size), half),
        ),
        in_specs=[vmem] * 6,
        out_specs=[anywhere] * 4 + [vmem],
        scratch_shapes=[
            pltpu.VMEM((key_count, head_size), half),
            pltpu.VMEM((key_count, 2 * head_size), half),
            pltpu.VMEM((tokens, columns), half),
            pltpu.VMEM((tokens, columns), half),
            pltpu.VMEM((2, tokens, head_size), half),
            pltpu.SemaphoreType.DMA((4,)),
        ],
        compiler_params=pltpu.CompilerParams(vmem_limit_bytes=48 * 1024 * 1024),
    )(living, queries[0], grad_out[0], resp_keys[0], resp_values[0], prefix)
    pieces = lax.all_to_all(share, "roll", 0, 0)
    total = pieces[0].astype(jnp.float32)
    for rank in range(1, ranks):
        total = total + pieces[rank].astype(jnp.float32)
    return (
        attended[None],
        query_grad[None],
        key_grad[None],
        value_grad[None],
        total[:, :head_size],
        total[:, head_size:],
    )


def solution(mesh):
    rolls = P(("prompt", "roll"), None, "head")
    prompts = P(("prompt", "roll"), "head")
    return jax.shard_map(
        functools.partial(on_device, mesh.shape["roll"]),
        mesh=mesh,
        in_specs=(rolls, rolls, rolls, prompts, prompts, rolls, P(("prompt", "roll"))),
        out_specs=(rolls, rolls, rolls, rolls, prompts, prompts),
        check_vma=False,
    )
```

time: 44.4 us -> 40.7 us (0.917)
  blocking collectives: 13.5 us -> 32.8 us
  starting transfers between devices: 10.4 us -> 0 us
  waiting for transfers between devices: 9.23 us -> 0 us
  Pallas kernels: 7.27 us -> 5.42 us
  local copies, waits for them, and re-layouts: 1.49 us -> 0.66 us
  other arithmetic: 0.82 us -> 0.07 us
    all_to_all x0 -> x1, blocking collectives: none -> 19.3 us  [on_device(): prefix = lax.all_to_all(sent, 'roll', 0, 0)]
    all_to_all x1 -> x0, starting transfers between devices: 10.4 us -> none  [on_device(): prefix = lax.all_to_all(sent, 'roll', 0, 0)]
    all_to_all x1 -> x0, waiting for transfers between devices: 9.23 us -> none  [on_device(): prefix = lax.all_to_all(sent, 'roll', 0, 0)]
    pallas_call x1 -> x2, Pallas kernels: 7.27 us -> 5.42 us  [the longest x1 4.6 us: on_device(): pl.pallas_call(attention_kernel, out_shape=(jax.ShapeDtypeStruct((tokens,...]
    broadcast_in_dim x1 -> x0, local copies, waits for them, and re-layouts: 0.84 us -> none  [on_device(): sent = jnp.broadcast_to(own[None], (ranks, *own.shape))]
    concatenate x1 -> x0, other arithmetic: 0.74 us -> none  [on_device(): own = jnp.concatenate([prefix_keys, prefix_values], axis=1)]
  transfers between devices with their start and end apart: 1 -> 0, of which waited for: 1 -> 0; matrix products, arithmetic and copies ran while one was open for 0% -> 0% of each run, Pallas kernels for 0% -> 0%
where the time goes in v3:
time: 40.7 us; the launch traced here: 40.3 us
  blocking collectives  32.8 us (81%)
  Pallas kernels  5.42 us (13%)
  between operations  1.34 us (3%)
  local copies, waits for them, and re-layouts  0.66 us (2%)
    all_to_all x1, blocking collectives, on_device(): prefix = lax.all_to_all(sent, 'roll', 0, 0)  19.3 us
    all_to_all x1, blocking collectives, on_device(): pieces = lax.all_to_all(share, 'roll', 0, 0)  13.5 us
    pallas_call x1, Pallas kernels, on_device(): pl.pallas_call(attention_kernel, out_shape=(jax.ShapeDtypeStruct((tokens,...  4.6 us
    pallas_call x1, Pallas kernels, on_device(): pl.pallas_call(spread_kernel, out_shape=(pltpu.VMEM((ranks, owned, 2 * he...  0.82 us

profile of v3, /device:TPU:1, one launch (start us, length us, event | category | flops | bytes accessed | tf_op | source)
XLA Modules:
  0.0 40.3 jit_solution(4837666912477255759)
XLA Ops:
  1.3 0.8 %shard_map.118 = (bf16[16,64,256]{2,1,0:T(8,128)(2,1)S(1)}, f32[128,128]{1,0:T(8,128)S(1)}) custom-call(s32[1]{0:T(128)S(6)} %copy.13.length_ref, bf16[64,128]{1,0:T(8,128)(2,1)} %key_hbm.1, bf16[64,128]{1,0:T(8,128)(2,1)} %value_hbm.1), custom_call_target="tpu_custom_call" | custom-call | tf_op jit(solution)/shard_map/pallas_call | solution.py:160
  2.1 0.0 copy-start
  2.1 0.0 copy-start.1
  2.1 0.0 copy-start.2
  2.1 0.0 copy-start.3
  2.2 19.3 %all_to_all.10.prefix_ref = bf16[16,64,256]{2,1,0:T(8,128)(2,1)S(1)} all-to-all(bf16[16,64,256]{2,1,0:T(8,128)(2,1)S(1)} %get-tuple-element.14), channel_id=1, replica_groups=mesh['prompt'=8,'roll'=16,'head'=4] {'roll'}, dimensions={0} | all-to-all | bytes 1048576 | tf_op jit(solution)/shard_map/all_to_all | solution.py:170
  21.5 0.0 copy-done
  21.5 0.0 copy-done.1
  21.5 0.0 copy-done.2
  21.5 0.0 copy-done.3
  21.5 4.6 %shard_map.119 = (bf16[128,1024]{1,0:T(8,128)(2,1)}, bf16[128,1024]{1,0:T(8,128)(2,1)}, bf16[128,128]{1,0:T(8,128)(2,1)}, bf16[128,128]{1,0:T(8,128)(2,1)}, bf16[16,64,256]{2,1,0:T(8,128)(2,1)S(1)}) custom-call(f32[128,128]{1,0:T(8,128)S(1)} %get-tuple-element.13.living_ref, bf16[128,1024]{1,0:T(8,128)(2,1)S(1)} %bitcast.15, bf16[128,1024]{1,0:T(8,128)(2,1)S(1)} %bitcast.16, ...), custom_call_target="tpu_custom_call" | custom-call | tf_op jit(solution)/shard_map/pallas_call | solution.py:171
  26.1 13.5 %all_to_all.11 = bf16[16,64,256]{2,1,0:T(8,128)(2,1)S(1)} all-to-all(bf16[16,64,256]{2,1,0:T(8,128)(2,1)S(1)} %get-tuple-element.19), channel_id=1, replica_groups=mesh['prompt'=8,'roll'=16,'head'=4] {'roll'}, dimensions={0} | all-to-all | bytes 1048576 | tf_op jit(solution)/shard_map/all_to_all | solution.py:192
  39.6 0.1 convert_add_fusion
  39.7 0.6 %fusion = (f32[64,128]{1,0:T(8,128)}, f32[64,128]{1,0:T(8,128)}) fusion(f32[64,256]{1,0:T(8,128)S(1)} %convert_add_fusion), kind=kLoop, calls=%fused_computation.2 | loop fusion | bytes 131072 | tf_op jit(solution)/shard_map/slice | solution.py:202
Async XLA Ops:
  2.1 19.4 %copy-start = (bf16[1,128,1024]{2,1,0:T(8,128)(2,1)S(1)}, bf16[1,128,1024]{2,1,0:T(8,128)(2,1)}, u32[]{:S(2)}) copy-start(bf16[1,128,1024]{2,1,0:T(8,128)(2,1)} %param.7) | copy-start | bytes 786436
  2.1 19.4 %copy-start.1 = (bf16[1,128,1024]{2,1,0:T(8,128)(2,1)S(1)}, bf16[1,128,1024]{2,1,0:T(8,128)(2,1)}, u32[]{:S(2)}) copy-start(bf16[1,128,1024]{2,1,0:T(8,128)(2,1)} %param.12) | copy-start | bytes 786436
  2.1 19.4 %copy-start.2 = (bf16[1,128,128]{2,1,0:T(8,128)(2,1)S(1)}, bf16[1,128,128]{2,1,0:T(8,128)(2,1)}, u32[]{:S(2)}) copy-start(bf16[1,128,128]{2,1,0:T(8,128)(2,1)} %param.8) | copy-start | bytes 98308
  2.1 19.4 %copy-start.3 = (bf16[1,128,128]{2,1,0:T(8,128)(2,1)S(1)}, bf16[1,128,128]{2,1,0:T(8,128)(2,1)}, u32[]{:S(2)}) copy-start(bf16[1,128,128]{2,1,0:T(8,128)(2,1)} %param.9) | copy-start | bytes 98308

commit v4 on v3

v4 whole, which is shorter than its diff:
```python
import functools
import math

import jax
import jax.numpy as jnp
from jax import lax
from jax.experimental import pallas as pl
from jax.experimental.pallas import tpu as pltpu
from jax.sharding import PartitionSpec as P

masked_score = -1e30
GROUP = 4


def contract(left, right, dims):
    return lax.dot_general(
        left, right, ((dims[:1], dims[1:]), ((), ())), preferred_element_type=jnp.float32
    )


def head_parts(columns, tokens, head_size):
    return [
        (slice(head * tokens, (head + 1) * tokens), slice(head * head_size, (head + 1) * head_size))
        for head in range(columns // head_size)
    ]


def spread_kernel(length_ref, key_hbm, value_hbm, out_ref, living_ref, own, sems):
    head_size = key_hbm.shape[1]
    copies = [
        pltpu.make_async_copy(source, own.at[place], sems.at[place])
        for place, source in enumerate((key_hbm, value_hbm))
    ]
    for copy in copies:
        copy.start()
    token = lax.broadcasted_iota(jnp.int32, living_ref.shape, 0)
    living_ref[...] = (token < length_ref[0]).astype(jnp.float32)
    for copy in copies:
        copy.wait()
    for place in range(out_ref.shape[0]):
        out_ref[place, :, :head_size] = own[0]
        out_ref[place, :, head_size:] = own[1]


def near_kernel(
    query_hbm,
    grad_hbm,
    resp_key_hbm,
    resp_value_hbm,
    near_ref,
    query_rows_ref,
    grad_ref,
    own_ref,
    scores_ref,
    query_ref,
    sems,
):
    tokens, head_size = own_ref.shape[1:]
    moves = (
        (query_hbm, query_ref),
        (grad_hbm, grad_ref),
        (resp_key_hbm, own_ref.at[0]),
        (resp_value_hbm, own_ref.at[1]),
    )
    copies = [
        pltpu.make_async_copy(source, target, sems.at[place])
        for place, (source, target) in enumerate(moves)
    ]
    for copy in copies:
        copy.start()
    keys = jnp.concatenate([near_ref[place, :, :head_size] for place in range(near_ref.shape[0])], axis=0)
    copies[0].wait()
    for rows, span in head_parts(query_ref.shape[1], tokens, head_size):
        query = query_ref[:, span]
        query_rows_ref[rows] = query
        scores_ref[rows] = contract(query, keys, (1, 1))
    for copy in copies[1:]:
        copy.wait()


def attention_kernel(
    living_ref,
    query_rows_ref,
    grad_ref,
    own_ref,
    near_ref,
    far_ref,
    near_scores_ref,
    attended_hbm,
    weights_ref,
    grad_scores_ref,
    grad_rows_ref,
    key_rows,
    far_share_ref,
    value_rows,
    attended_ref,
    sem,
):
    tokens, head_size = own_ref.shape[1:]
    chips, owned, _ = near_ref.shape
    half = chips * owned
    prompt = 2 * half
    heads = grad_ref.shape[1] // head_size
    factor = 1.0 / math.sqrt(head_size)
    exponent_factor = factor * math.log2(math.e)
    parts = head_parts(grad_ref.shape[1], tokens, head_size)
    for side, part_ref in enumerate((near_ref, far_ref)):
        for chip in range(chips):
            span = slice(side * half + chip * owned, side * half + (chip + 1) * owned)
            key_rows[span] = part_ref[chip, :, :head_size]
            value_rows[span, :head_size] = part_ref[chip, :, head_size:]
    key_rows[prompt:] = own_ref[0]
    value_rows[prompt:, :head_size] = own_ref[1]
    value_rows[:, head_size:] = jnp.ones((prompt + tokens, head_size), jnp.bfloat16)

    groups = [parts[at : at + GROUP] for at in range(0, heads, GROUP)]
    queries = [query_rows_ref[at * tokens : (at + GROUP) * tokens] for at in range(0, heads, GROUP)]
    grads = [jnp.concatenate([grad_ref[:, span] for _, span in group], axis=0) for group in groups]
    living = jnp.concatenate([living_ref[...]] * GROUP, axis=0) > 0.0
    token = lax.broadcasted_iota(jnp.int32, (GROUP * tokens, tokens), 0) % tokens
    allowed = lax.broadcasted_iota(jnp.int32, (GROUP * tokens, tokens), 1) <= token

    def exponentials(near, scores):
        own = jnp.where(allowed, scores[:, half:], masked_score)
        parts = (near, scores[:, :half], own)
        row_max = functools.reduce(jnp.maximum, [jnp.max(part, axis=1, keepdims=True) for part in parts])
        return jnp.concatenate(
            [jnp.exp2((part - row_max) * exponent_factor).astype(jnp.bfloat16) for part in parts], axis=1
        )

    def normalised(index, sums):
        inverse = 1.0 / sums[:, head_size:]
        outputs = sums[:, :head_size] * inverse
        attended = jnp.where(living, outputs, 0.0).astype(jnp.bfloat16)
        for place, (_, span) in enumerate(groups[index]):
            attended_ref[:, span] = attended[place * tokens : (place + 1) * tokens]
        grad = jnp.where(living, grads[index].astype(jnp.float32) * inverse, 0.0).astype(jnp.bfloat16)
        return grad, jnp.sum(grad.astype(jnp.float32) * outputs, axis=1, keepdims=True)

    count = len(groups)
    scores, weights, sums, states, grad_weights, grad_scores = ([None] * count for _ in range(6))

    def score(index):
        scores[index] = contract(queries[index], key_rows[half:], (1, 1))

    def weigh(index):
        rows = slice(index * GROUP * tokens, (index + 1) * GROUP * tokens)
        weights[index] = exponentials(near_scores_ref[rows], scores[index])

    def attend(index):
        sums[index] = contract(weights[index], value_rows[...], (1, 0))

    def normalise(index):
        states[index] = normalised(index, sums[index])

    def grad_weigh(index):
        grad_weights[index] = contract(states[index][0], value_rows[:, :head_size], (1, 1))

    def grad_score(index):
        shifted = (grad_weights[index] - states[index][1]).astype(jnp.bfloat16)
        grad_scores[index] = weights[index] * shifted

    for step in range(count + 1):
        if step < count:
            score(step)
        if step > 0:
            weigh(step - 1)
            attend(step - 1)
    for step in range(count + 1):
        if step < count:
            normalise(step)
            grad_weigh(step)
        if step > 0:
            grad_score(step - 1)
    copy = pltpu.make_async_copy(attended_ref, attended_hbm, sem)
    copy.start()
    query = query_rows_ref[...]
    grad = jnp.concatenate([state[0] for state in states], axis=0)
    grad_rows_ref[...] = grad
    weights = jnp.concatenate(weights, axis=0)
    weights_ref[...] = weights
    grad_scores = jnp.concatenate(grad_scores, axis=0)
    grad_scores_ref[...] = grad_scores
    key_total = (contract(query, grad_scores[:, half:prompt], (0, 0)) * factor).astype(jnp.bfloat16).T
    value_total = contract(grad, weights[:, half:prompt], (0, 0)).astype(jnp.bfloat16).T
    for chip in range(chips):
        span = slice(chip * owned, (chip + 1) * owned)
        far_share_ref[chip, :, :head_size] = key_total[span]
        far_share_ref[chip, :, head_size:] = value_total[span]
    copy.wait()


def finish_kernel(
    query_rows_ref,
    weights_ref,
    grad_scores_ref,
    grad_rows_ref,
    key_rows,
    query_grad_hbm,
    key_grad_hbm,
    value_grad_hbm,
    near_share_ref,
    query_grad_ref,
    own_grad_ref,
    sems,
):
    tokens, head_size = own_grad_ref.shape[1:]
    half = near_share_ref.shape[0]
    prompt = 2 * half
    factor = 1.0 / math.sqrt(head_size)
    parts = head_parts(query_grad_ref.shape[1], tokens, head_size)
    copies = []

    def send(source, target):
        copy = pltpu.make_async_copy(source, target, sems.at[len(copies)])
        copy.start()
        copies.append(copy)

    query_grad = (contract(grad_scores_ref[...], key_rows[...], (1, 0)) * factor).astype(jnp.bfloat16)
    for rows, span in parts:
        query_grad_ref[:, span] = query_grad[rows]
    send(query_grad_ref, query_grad_hbm)
    query = query_rows_ref[...]
    operands = ((query, grad_scores_ref, factor), (grad_rows_ref[...], weights_ref, 1.0))
    for place, (rows, columns, scale) in enumerate(operands):
        own = contract(rows, columns[:, prompt:], (0, 0)) * scale
        own_grad_ref[place] = own.astype(jnp.bfloat16).T
        send(own_grad_ref.at[place], (key_grad_hbm, value_grad_hbm)[place])
    for place, (rows, columns, scale) in enumerate(operands):
        near = contract(rows, columns[:, :half], (0, 0)) * scale
        near_share_ref[:, place * head_size : (place + 1) * head_size] = near.T
    for copy in copies:
        copy.wait()


def join_kernel(near_share_ref, received_ref, out_ref):
    chips, owned, _ = out_ref.shape
    for chip in range(chips):
        near = near_share_ref[chip * owned : (chip + 1) * owned]
        out_ref[chip] = (near + received_ref[chip].astype(jnp.float32)).astype(jnp.bfloat16)


def on_device(ranks, queries, resp_keys, resp_values, prefix_keys, prefix_values, grad_out, lengths):
    tokens, columns = queries.shape[1:]
    owned, head_size = prefix_keys.shape
    key_count = ranks * owned + tokens
    half = jnp.bfloat16
    vmem = pl.BlockSpec(memory_space=pltpu.VMEM)
    anywhere = pl.BlockSpec(memory_space=pl.ANY)

    sent, living = pl.pallas_call(
        spread_kernel,
        out_shape=(
            pltpu.VMEM((ranks // 2, owned, 2 * head_size), half),
            pltpu.VMEM((tokens, head_size), jnp.float32),
        ),
        in_specs=[pl.BlockSpec(memory_space=pltpu.SMEM)] + [pl.BlockSpec(memory_space=pltpu.HBM)] * 2,
        out_specs=[vmem] * 2,
        scratch_shapes=[pltpu.VMEM((2, owned, head_size), half), pltpu.SemaphoreType.DMA((2,))],
    )(lengths, *(pltpu.with_memory_space_constraint(array, pltpu.HBM) for array in (prefix_keys, prefix_values)))
    same_core = [list(range(core, ranks, 2)) for core in range(2)]
    near = lax.all_to_all(sent, "roll", 0, 0, axis_index_groups=same_core)
    far = lax.ppermute(near, "roll", [(rank, rank ^ 1) for rank in range(ranks)])
    rows = columns // head_size * tokens
    hbm = pl.BlockSpec(memory_space=pltpu.HBM)
    stored = (queries[0], grad_out[0], resp_keys[0], resp_values[0])
    query_rows, grads, own, near_scores = pl.pallas_call(
        near_kernel,
        out_shape=(
            pltpu.VMEM((rows, head_size), half),
            pltpu.VMEM((tokens, columns), half),
            pltpu.VMEM((2, tokens, head_size), half),
            pltpu.VMEM((rows, ranks * owned // 2), jnp.float32),
        ),
        in_specs=[hbm] * 4 + [vmem],
        out_specs=[vmem] * 4,
        scratch_shapes=[pltpu.VMEM((tokens, columns), half), pltpu.SemaphoreType.DMA((4,))],
        compiler_params=pltpu.CompilerParams(vmem_limit_bytes=24 * 1024 * 1024),
        cost_estimate=pl.CostEstimate(
            flops=rows * ranks * owned * head_size, bytes_accessed=4 * rows * head_size, transcendentals=0
        ),
    )(*(pltpu.with_memory_space_constraint(array, pltpu.HBM) for array in stored), near)
    limit = pltpu.CompilerParams(vmem_limit_bytes=40 * 1024 * 1024)
    unit = 2 * rows * key_count * head_size
    chips = ranks // 2
    attended, weights, grad_scores, grad_rows, key_rows, far_share = pl.pallas_call(
        attention_kernel,
        out_shape=(
            jax.ShapeDtypeStruct((tokens, columns), half),
            pltpu.VMEM((rows, key_count), half),
            pltpu.VMEM((rows, key_count), half),
            pltpu.VMEM((rows, head_size), half),
            pltpu.VMEM((key_count, head_size), half),
            pltpu.VMEM((chips, owned, 2 * head_size), half),
        ),
        in_specs=[vmem] * 7,
        out_specs=[anywhere] + [vmem] * 5,
        scratch_shapes=[
            pltpu.VMEM((key_count, 2 * head_size), half),
            pltpu.VMEM((tokens, columns), half),
            pltpu.SemaphoreType.DMA,
        ],
        compiler_params=limit,
        cost_estimate=pl.CostEstimate(flops=5 * unit, bytes_accessed=4 * rows * columns, transcendentals=0),
    )(living, query_rows, grads, own, near, far, near_scores)
    received = lax.ppermute(far_share, "roll", [(rank, rank ^ 1) for rank in range(ranks)])
    query_grad, key_grad, value_grad, near_share = pl.pallas_call(
        finish_kernel,
        out_shape=(
            jax.ShapeDtypeStruct((tokens, columns), half),
            jax.ShapeDtypeStruct((tokens, head_size), half),
            jax.ShapeDtypeStruct((tokens, head_size), half),
            pltpu.VMEM((chips * owned, 2 * head_size), jnp.float32),
        ),
        in_specs=[vmem] * 5,
        out_specs=[anywhere] * 3 + [vmem],
        scratch_shapes=[
            pltpu.VMEM((tokens, columns), half),
            pltpu.VMEM((2, tokens, head_size), half),
            pltpu.SemaphoreType.DMA((3,)),
        ],
        compiler_params=limit,
        cost_estimate=pl.CostEstimate(flops=2 * unit, bytes_accessed=4 * rows * columns, transcendentals=0),
    )(query_rows, weights, grad_scores, grad_rows, key_rows)
    share = pl.pallas_call(
        join_kernel,
        out_shape=pltpu.VMEM((chips, owned, 2 * head_size), half),
        in_specs=[vmem] * 2,
        out_specs=vmem,
    )(near_share, received)
    pieces = lax.all_to_all(share, "roll", 0, 0, axis_index_groups=same_core)
    total = pieces[0].astype(jnp.float32)
    for chip in range(1, chips):
        total = total + pieces[chip].astype(jnp.float32)
    return (
        attended[None],
        query_grad[None],
        key_grad[None],
        value_grad[None],
        total[:, :head_size],
        total[:, head_size:],
    )


def solution(mesh):
    rolls = P(("prompt", "roll"), None, "head")
    prompts = P(("prompt", "roll"), "head")
    return jax.shard_map(
        functools.partial(on_device, mesh.shape["roll"]),
        mesh=mesh,
        in_specs=(rolls, rolls, rolls, prompts, prompts, rolls, P(("prompt", "roll"))),
        out_specs=(rolls, rolls, rolls, rolls, prompts, prompts),
        check_vma=False,
    )
```

time: 40.7 us -> 41.2 us (1.012)
  blocking collectives: 32.8 us -> 21.6 us
  starting transfers between devices: 0 us -> 7.85 us
  Pallas kernels: 5.42 us -> 7.86 us
  local copies, waits for them, and re-layouts: 0.66 us -> 2.13 us
    all_to_all x2, blocking collectives: 32.8 us -> 21.6 us  [the longest x1 12.6 us: on_device(): near = lax.all_to_all(sent, 'roll', 0, 0, axis_index_groups=same_core)]
    ppermute x0 -> x2, starting transfers between devices: none -> 7.85 us  [the longest x1 5.88 us: on_device(): lax.ppermute(near, 'roll', [(rank, rank ^ 1) for rank in range(ranks)])]
    pallas_call x1 -> x4, Pallas kernels: 0.82 us -> 5.3 us  [the longest x1 1.93 us: on_device(): pl.pallas_call(finish_kernel, out_shape=(jax.ShapeDtypeStruct((tokens, co...]
    pallas_call x1, Pallas kernels: 4.6 us -> 2.55 us  [on_device(): pl.pallas_call(attention_kernel, out_shape=(jax.ShapeDtypeStruct((tokens,...]
    unnamed x8 -> x4, local copies, waits for them, and re-layouts: 0.03 us -> 1.5 us
  transfers between devices with their start and end apart: 0 -> 2, of which waited for: 0 -> 0; matrix products, arithmetic and copies ran while one was open for 0% -> 0% of each run, Pallas kernels for 0% -> 8%
where the time goes in v4:
time: 41.2 us; the launch traced here: 40.8 us
  blocking collectives  21.6 us (52%)
  Pallas kernels  7.86 us (19%)
  starting transfers between devices  7.85 us (19%)
  local copies, waits for them, and re-layouts  2.13 us (5%)
  between operations  1.35 us (3%)
    all_to_all x1, blocking collectives, on_device(): near = lax.all_to_all(sent, 'roll', 0, 0, axis_index_groups=same_core)  12.6 us
    all_to_all x1, blocking collectives, on_device(): pieces = lax.all_to_all(share, 'roll', 0, 0, axis_index_groups=same_core)  8.99 us
    ppermute x1, starting transfers between devices, on_device(): lax.ppermute(near, 'roll', [(rank, rank ^ 1) for rank in range(ranks)])  5.88 us
    pallas_call x1, Pallas kernels, on_device(): pl.pallas_call(attention_kernel, out_shape=(jax.ShapeDtypeStruct((tokens,...  2.55 us
    ppermute x1, starting transfers between devices, on_device(): lax.ppermute(far_share, 'roll', [(rank, rank ^ 1) for rank in range(ranks)])  1.97 us
    pallas_call x1, Pallas kernels, on_device(): pl.pallas_call(finish_kernel, out_shape=(jax.ShapeDtypeStruct((tokens, co...  1.93 us
    unnamed x4, local copies, waits for them, and re-layouts  1.5 us
    pallas_call x1, Pallas kernels, on_device(): pl.pallas_call(near_kernel, out_shape=(pltpu.VMEM((rows, head_size), half...  1.43 us
  transfers between devices with their start and end apart: 2, of which 0 were waited for; matrix products, arithmetic and copies ran while one was open for 0% of the time, Pallas kernels for 8%

profile of v4, /device:TPU:1, one launch (start us, length us, event | category | flops | bytes accessed | tf_op | source)
XLA Modules:
  0.0 40.8 jit_solution(17912380879201554138)
XLA Ops:
  1.3 0.8 %shard_map.118 = (bf16[8,64,256]{2,1,0:T(8,128)(2,1)S(1)}, f32[128,128]{1,0:T(8,128)S(1)}) custom-call(s32[1]{0:T(128)S(6)} %copy.13.length_ref, bf16[64,128]{1,0:T(8,128)(2,1)} %key_hbm.1, bf16[64,128]{1,0:T(8,128)(2,1)} %value_hbm.1), custom_call_target="tpu_custom_call" | custom-call | tf_op jit(solution)/shard_map/pallas_call | solution.py:251
  2.1 12.6 %all_to_all.10.near_ref = bf16[8,64,256]{2,1,0:T(8,128)(2,1)S(1)} all-to-all(bf16[8,64,256]{2,1,0:T(8,128)(2,1)S(1)} %get-tuple-element.23), channel_id=1, replica_groups={{0,8,16,24,32,40,48,56},{4,12,20,28,36,44,52,60},{1,9,17,25,33,41,49,57..., dimensions={0} | all-to-all | bytes 524288 | tf_op jit(solution)/shard_map/all_to_all | solution.py:262
  14.7 5.9 %collective-permute-start = (bf16[8,64,256]{2,1,0:T(8,128)(2,1)S(1)}, bf16[8,64,256]{2,1,0:T(8,128)(2,1)S(1)}, u32[]{:S(2)}, u32[]{:S(2)}) collective-permute-start(bf16[8,64,256]{2,1,0:T(8,128)(2,1)S(1)} %all_to_all.10.near_ref), channel_id=1, source_target_pairs={{0,4},{4,0},{8,12},{12,8},{16,20},{20,16},{24,28},{28,24},{32,36},... | collective-permute-start | bytes 786440 | tf_op jit(solution)/shard_map/ppermute | solution.py:263
  20.6 1.4 %shard_map.119 = (bf16[1024,128]{1,0:T(8,128)(2,1)S(1)}, bf16[128,1024]{1,0:T(8,128)(2,1)S(1)}, bf16[2,128,128]{2,1,0:T(8,128)(2,1)S(1)}, f32[1024,512]{1,0:T(8,128)S(1)}) custom-call(bf16[128,1024]{1,0:T(8,128)(2,1)} %bitcast.10, bf16[128,1024]{1,0:T(8,128)(2,1)} %bitcast.11, bf16[128,128]{1,0:T(8,128)(2,1)} %bitcast.12, bf16[128,128]{1,0:T(8,128)(2,1)} %bitcast.13, ...), custom_call_target="tpu_custom_call" | custom-call | flops 134217728 | bytes 524288 | tf_op jit(solution)/shard_map/pallas_call | solution.py:267
  22.0 0.0 collective-permute-done.far_ref
  22.0 2.6 %shard_map.120 = (bf16[128,1024]{1,0:T(8,128)(2,1)}, bf16[1024,1152]{1,0:T(8,128)(2,1)S(1)}, bf16[1024,1152]{1,0:T(8,128)(2,1)S(1)}, bf16[1024,128]{1,0:T(8,128)...) custom-call(f32[128,128]{1,0:T(8,128)S(1)} %get-tuple-element.22.living_ref, ...), custom_call_target="tpu_custom_call" | custom-call | flops 1509949440 | bytes 4194304 | tf_op jit(solution)/shard_map/pallas_call | solution.py:286
  24.6 2.0 %collective-permute-start.1 = (bf16[8,64,256]{2,1,0:T(8,128)(2,1)S(1)}, bf16[8,64,256]{2,1,0:T(8,128)(2,1)S(1)}, u32[]{:S(2)}, u32[]{:S(2)}) collective-permute-start(bf16[8,64,256]{2,1,0:T(8,128)(2,1)S(1)} %get-tuple-element.37), channel_id=1, source_target_pairs={{0,4},{4,0},{8,12},{12,8},{16,20},{20,16},{24,28},{28,24},{32,36},... | collective-permute-start | bytes 786440 | tf_op jit(solution)/shard_map/ppermute | solution.py:306
  26.5 1.9 %shard_map.121 = (bf16[128,1024]{1,0:T(8,128)(2,1)}, bf16[128,128]{1,0:T(8,128)(2,1)}, bf16[128,128]{1,0:T(8,128)(2,1)}, f32[512,256]{1,0:T(8,128)S(1)}) custom-call(bf16[1024,128]{1,0:T(8,128)(2,1)S(1)} %get-tuple-element.24.query_rows_ref, bf16[1024,1152]{1,0:T(8,128)(2,1)S(1)} %get-tuple-element.29.weights_ref, ...), custom_call_target="tpu_custom_call" | custom-call | flops 603979776 | bytes 4194304 | tf_op jit(solution)/shard_map/pallas_call | solution.py:307
  28.5 0.0 copy-start
  28.5 0.8 %copy-done = f32[512,256]{1,0:T(8,128)} copy-done((f32[512,256]{1,0:T(8,128)}, f32[512,256]{1,0:T(8,128)S(1)}, u32[]{:S(2)}) %copy-start) | copy-done | bytes 524312
  29.3 0.0 collective-permute-done.1.received_ref
  29.3 0.0 copy-start.1
  29.3 0.7 %copy-done.1 = bf16[8,64,256]{2,1,0:T(8,128)(2,1)} copy-done((bf16[8,64,256]{2,1,0:T(8,128)(2,1)}, bf16[8,64,256]{2,1,0:T(8,128)(2,1)S(1)}, u32[]{:S(2)}) %copy-start.1) | copy-done | bytes 262168
  30.0 1.2 %shard_map.122 = bf16[8,64,256]{2,1,0:T(8,128)(2,1)S(1)} custom-call(f32[512,256]{1,0:T(8,128)} %copy-done, bf16[8,64,256]{2,1,0:T(8,128)(2,1)} %copy-done.1), custom_call_target="tpu_custom_call" | custom-call | tf_op jit(solution)/shard_map/pallas_call | solution.py:325
  31.2 9.0 %all_to_all.11 = bf16[8,64,256]{2,1,0:T(8,128)(2,1)S(1)} all-to-all(bf16[8,64,256]{2,1,0:T(8,128)(2,1)S(1)} %shard_map.122), channel_id=1, replica_groups={{0,8,16,24,32,40,48,56},{4,12,20,28,36,44,52,60},{1,9,17,25,33,41,49,57..., dimensions={0} | all-to-all | bytes 524288 | tf_op jit(solution)/shard_map/all_to_all | solution.py:331
  40.2 0.6 %fusion = (f32[64,128]{1,0:T(8,128)}, f32[64,128]{1,0:T(8,128)}) fusion(f32[64,256]{1,0:T(8,128)S(1)} %add_bitcast_fusion), kind=kLoop, calls=%fused_computation.1 | loop fusion | bytes 131072 | tf_op jit(solution)/shard_map/slice | solution.py:341
  (1 shorter events, 0.0 us)
Async XLA Ops:
  14.7 7.3 %collective-permute-start = (bf16[8,64,256]{2,1,0:T(8,128)(2,1)S(1)}, bf16[8,64,256]{2,1,0:T(8,128)(2,1)S(1)}, u32[]{:S(2)}, u32[]{:S(2)}) collective-permute-start(bf16[8,64,256]{2,1,0:T(8,128)(2,1)S(1)} %all_to_all.10.near_ref), channel_id=1, source_target_pairs={{0,4},{4,0},{8,12},{12,8},{16,20},{20,16},{24,28},{28,24},{32,36},... | collective-permute-start | bytes 786440 | tf_op jit(solution)/shard_map/ppermute | solution.py:263
  24.6 4.7 %collective-permute-start.1 = (bf16[8,64,256]{2,1,0:T(8,128)(2,1)S(1)}, bf16[8,64,256]{2,1,0:T(8,128)(2,1)S(1)}, u32[]{:S(2)}, u32[]{:S(2)}) collective-permute-start(bf16[8,64,256]{2,1,0:T(8,128)(2,1)S(1)} %get-tuple-element.37), channel_id=1, source_target_pairs={{0,4},{4,0},{8,12},{12,8},{16,20},{20,16},{24,28},{28,24},{32,36},... | collective-permute-start | bytes 786440 | tf_op jit(solution)/shard_map/ppermute | solution.py:306
  28.5 0.8 %copy-start = (f32[512,256]{1,0:T(8,128)}, f32[512,256]{1,0:T(8,128)S(1)}, u32[]{:S(2)}) copy-start(f32[512,256]{1,0:T(8,128)S(1)} %get-tuple-element.36.near_share_ref) | copy-start | bytes 1572868
  29.3 0.7 %copy-start.1 = (bf16[8,64,256]{2,1,0:T(8,128)(2,1)}, bf16[8,64,256]{2,1,0:T(8,128)(2,1)S(1)}, u32[]{:S(2)}) copy-start(bf16[8,64,256]{2,1,0:T(8,128)(2,1)S(1)} %collective-permute-done.1.received_ref) | copy-start | bytes 786436

commit v5 on v4

--- a/solution.py
+++ b/solution.py
@@ -327,6 +327,7 @@
         out_shape=pltpu.VMEM((chips, owned, 2 * head_size), half),
         in_specs=[vmem] * 2,
         out_specs=vmem,
+        compiler_params=pltpu.CompilerParams(vmem_limit_bytes=8 * 1024 * 1024),
     )(near_share, received)
     pieces = lax.all_to_all(share, "roll", 0, 0, axis_index_groups=same_core)
     total = pieces[0].astype(jnp.float32)

time: 41.2 us -> 38.6 us (0.937)
  local copies, waits for them, and re-layouts: 2.13 us -> 0.63 us
  Pallas kernels: 7.86 us -> 6.75 us
    unnamed x4 -> x0, local copies, waits for them, and re-layouts: 1.5 us -> none
    pallas_call x1, Pallas kernels: 1.15 us -> 0.05 us  [on_device(): pl.pallas_call(join_kernel, out_shape=pltpu.VMEM((chips, owned, 2 * head_...]
  transfers between devices with their start and end apart: 2 -> 2, of which waited for: 0 -> 0; matrix products, arithmetic and copies ran while one was open for 0% -> 0% of each run, Pallas kernels for 8% -> 9%
where the time goes in v5:
time: 38.6 us; the launch traced here: 38.2 us
  blocking collectives  21.6 us (56%)
  starting transfers between devices  7.85 us (20%)
  Pallas kernels  6.75 us (17%)
  between operations  1.35 us (3%)
  local copies, waits for them, and re-layouts  0.63 us (2%)
    all_to_all x1, blocking collectives, on_device(): near = lax.all_to_all(sent, 'roll', 0, 0, axis_index_groups=same_core)  12.6 us
    all_to_all x1, blocking collectives, on_device(): pieces = lax.all_to_all(share, 'roll', 0, 0, axis_index_groups=same_core)  8.99 us
    ppermute x1, starting transfers between devices, on_device(): lax.ppermute(near, 'roll', [(rank, rank ^ 1) for rank in range(ranks)])  5.88 us
    pallas_call x1, Pallas kernels, on_device(): pl.pallas_call(attention_kernel, out_shape=(jax.ShapeDtypeStruct((tokens,...  2.55 us
    ppermute x1, starting transfers between devices, on_device(): lax.ppermute(far_share, 'roll', [(rank, rank ^ 1) for rank in range(ranks)])  1.97 us
    pallas_call x1, Pallas kernels, on_device(): pl.pallas_call(finish_kernel, out_shape=(jax.ShapeDtypeStruct((tokens, co...  1.93 us
    pallas_call x1, Pallas kernels, on_device(): pl.pallas_call(near_kernel, out_shape=(pltpu.VMEM((rows, head_size), half...  1.43 us
    pallas_call x1, Pallas kernels, on_device(): pl.pallas_call(spread_kernel, out_shape=(pltpu.VMEM((ranks // 2, owned, 2...  0.79 us
  transfers between devices with their start and end apart: 2, of which 0 were waited for; matrix products, arithmetic and copies ran while one was open for 0% of the time, Pallas kernels for 9%

profile of v5, /device:TPU:1, one launch (start us, length us, event | category | flops | bytes accessed | tf_op | source)
XLA Modules:
  0.0 38.2 jit_solution(3811403327648123074)
XLA Ops:
  1.3 0.8 %shard_map.118 = (bf16[8,64,256]{2,1,0:T(8,128)(2,1)S(1)}, f32[128,128]{1,0:T(8,128)S(1)}) custom-call(s32[1]{0:T(128)S(6)} %copy.13.length_ref, bf16[64,128]{1,0:T(8,128)(2,1)} %key_hbm.1, bf16[64,128]{1,0:T(8,128)(2,1)} %value_hbm.1), custom_call_target="tpu_custom_call" | custom-call | tf_op jit(solution)/shard_map/pallas_call | solution.py:251
  2.1 12.6 %all_to_all.10.near_ref = bf16[8,64,256]{2,1,0:T(8,128)(2,1)S(1)} all-to-all(bf16[8,64,256]{2,1,0:T(8,128)(2,1)S(1)} %get-tuple-element.23), channel_id=1, replica_groups={{0,8,16,24,32,40,48,56},{4,12,20,28,36,44,52,60},{1,9,17,25,33,41,49,57..., dimensions={0} | all-to-all | bytes 524288 | tf_op jit(solution)/shard_map/all_to_all | solution.py:262
  14.7 5.9 %collective-permute-start = (bf16[8,64,256]{2,1,0:T(8,128)(2,1)S(1)}, bf16[8,64,256]{2,1,0:T(8,128)(2,1)S(1)}, u32[]{:S(2)}, u32[]{:S(2)}) collective-permute-start(bf16[8,64,256]{2,1,0:T(8,128)(2,1)S(1)} %all_to_all.10.near_ref), channel_id=1, source_target_pairs={{0,4},{4,0},{8,12},{12,8},{16,20},{20,16},{24,28},{28,24},{32,36},... | collective-permute-start | bytes 786440 | tf_op jit(solution)/shard_map/ppermute | solution.py:263
  20.6 1.4 %shard_map.119 = (bf16[1024,128]{1,0:T(8,128)(2,1)S(1)}, bf16[128,1024]{1,0:T(8,128)(2,1)S(1)}, bf16[2,128,128]{2,1,0:T(8,128)(2,1)S(1)}, f32[1024,512]{1,0:T(8,128)S(1)}) custom-call(bf16[128,1024]{1,0:T(8,128)(2,1)} %bitcast.10, bf16[128,1024]{1,0:T(8,128)(2,1)} %bitcast.11, bf16[128,128]{1,0:T(8,128)(2,1)} %bitcast.12, bf16[128,128]{1,0:T(8,128)(2,1)} %bitcast.13, ...), custom_call_target="tpu_custom_call" | custom-call | flops 134217728 | bytes 524288 | tf_op jit(solution)/shard_map/pallas_call | solution.py:267
  22.0 0.0 collective-permute-done.far_ref
  22.0 2.6 %shard_map.120 = (bf16[128,1024]{1,0:T(8,128)(2,1)}, bf16[1024,1152]{1,0:T(8,128)(2,1)S(1)}, bf16[1024,1152]{1,0:T(8,128)(2,1)S(1)}, bf16[1024,128]{1,0:T(8,128)...) custom-call(f32[128,128]{1,0:T(8,128)S(1)} %get-tuple-element.22.living_ref, ...), custom_call_target="tpu_custom_call" | custom-call | flops 1509949440 | bytes 4194304 | tf_op jit(solution)/shard_map/pallas_call | solution.py:286
  24.6 2.0 %collective-permute-start.1 = (bf16[8,64,256]{2,1,0:T(8,128)(2,1)S(1)}, bf16[8,64,256]{2,1,0:T(8,128)(2,1)S(1)}, u32[]{:S(2)}, u32[]{:S(2)}) collective-permute-start(bf16[8,64,256]{2,1,0:T(8,128)(2,1)S(1)} %get-tuple-element.37), channel_id=1, source_target_pairs={{0,4},{4,0},{8,12},{12,8},{16,20},{20,16},{24,28},{28,24},{32,36},... | collective-permute-start | bytes 786440 | tf_op jit(solution)/shard_map/ppermute | solution.py:306
  26.5 1.9 %shard_map.121 = (bf16[128,1024]{1,0:T(8,128)(2,1)}, bf16[128,128]{1,0:T(8,128)(2,1)}, bf16[128,128]{1,0:T(8,128)(2,1)}, f32[512,256]{1,0:T(8,128)S(1)}) custom-call(bf16[1024,128]{1,0:T(8,128)(2,1)S(1)} %get-tuple-element.24.query_rows_ref, bf16[1024,1152]{1,0:T(8,128)(2,1)S(1)} %get-tuple-element.29.weights_ref, ...), custom_call_target="tpu_custom_call" | custom-call | flops 603979776 | bytes 4194304 | tf_op jit(solution)/shard_map/pallas_call | solution.py:307
  28.5 0.0 collective-permute-done.1.received_ref
  28.5 9.0 %all_to_all.11 = bf16[8,64,256]{2,1,0:T(8,128)(2,1)S(1)} all-to-all(bf16[8,64,256]{2,1,0:T(8,128)(2,1)S(1)} %shard_map.122), channel_id=1, replica_groups={{0,8,16,24,32,40,48,56},{4,12,20,28,36,44,52,60},{1,9,17,25,33,41,49,57..., dimensions={0} | all-to-all | bytes 524288 | tf_op jit(solution)/shard_map/all_to_all | solution.py:332
  37.6 0.6 %fusion = (f32[64,128]{1,0:T(8,128)}, f32[64,128]{1,0:T(8,128)}) fusion(f32[64,256]{1,0:T(8,128)S(1)} %add_bitcast_fusion), kind=kLoop, calls=%fused_computation.1 | loop fusion | bytes 131072 | tf_op jit(solution)/shard_map/slice | solution.py:342
  (2 shorter events, 0.1 us)
Async XLA Ops:
  14.7 7.3 %collective-permute-start = (bf16[8,64,256]{2,1,0:T(8,128)(2,1)S(1)}, bf16[8,64,256]{2,1,0:T(8,128)(2,1)S(1)}, u32[]{:S(2)}, u32[]{:S(2)}) collective-permute-start(bf16[8,64,256]{2,1,0:T(8,128)(2,1)S(1)} %all_to_all.10.near_ref), channel_id=1, source_target_pairs={{0,4},{4,0},{8,12},{12,8},{16,20},{20,16},{24,28},{28,24},{32,36},... | collective-permute-start | bytes 786440 | tf_op jit(solution)/shard_map/ppermute | solution.py:263
  24.6 3.9 %collective-permute-start.1 = (bf16[8,64,256]{2,1,0:T(8,128)(2,1)S(1)}, bf16[8,64,256]{2,1,0:T(8,128)(2,1)S(1)}, u32[]{:S(2)}, u32[]{:S(2)}) collective-permute-start(bf16[8,64,256]{2,1,0:T(8,128)(2,1)S(1)} %get-tuple-element.37), channel_id=1, source_target_pairs={{0,4},{4,0},{8,12},{12,8},{16,20},{20,16},{24,28},{28,24},{32,36},... | collective-permute-start | bytes 786440 | tf_op jit(solution)/shard_map/ppermute | solution.py:306

commit v6 on v5

--- a/solution.py
+++ b/solution.py
@@ -216,16 +216,20 @@
         copy.start()
         copies.append(copy)
 
-    query_grad = (contract(grad_scores_ref[...], key_rows[...], (1, 0)) * factor).astype(jnp.bfloat16)
-    for rows, span in parts:
-        query_grad_ref[:, span] = query_grad[rows]
-    send(query_grad_ref, query_grad_hbm)
     query = query_rows_ref[...]
     operands = ((query, grad_scores_ref, factor), (grad_rows_ref[...], weights_ref, 1.0))
     for place, (rows, columns, scale) in enumerate(operands):
         own = contract(rows, columns[:, prompt:], (0, 0)) * scale
         own_grad_ref[place] = own.astype(jnp.bfloat16).T
         send(own_grad_ref.at[place], (key_grad_hbm, value_grad_hbm)[place])
+    for first in range(0, len(parts), GROUP):
+        group = parts[first : first + GROUP]
+        taken = slice(group[0][0].start, group[-1][0].stop)
+        query_grad = contract(grad_scores_ref[taken], key_rows[...], (1, 0)) * factor
+        for place, (_, span) in enumerate(group):
+            query_grad_ref[:, span] = query_grad[place * tokens : (place + 1) * tokens].astype(jnp.bfloat16)
+        lanes = slice(group[0][1].start, group[-1][1].stop)
+        send(query_grad_ref.at[:, lanes], query_grad_hbm.at[:, lanes])
     for place, (rows, columns, scale) in enumerate(operands):
         near = contract(rows, columns[:, :half], (0, 0)) * scale
         near_share_ref[:, place * head_size : (place + 1) * head_size] = near.T
@@ -317,7 +321,7 @@
         scratch_shapes=[
             pltpu.VMEM((tokens, columns), half),
             pltpu.VMEM((2, tokens, head_size), half),
-            pltpu.SemaphoreType.DMA((3,)),
+            pltpu.SemaphoreType.DMA((2 + rows // tokens // GROUP,)),
         ],
         compiler_params=limit,
         cost_estimate=pl.CostEstimate(flops=2 * unit, bytes_accessed=4 * rows * columns, transcendentals=0),

time: 38.6 us -> 38.3 us (level)
  transfers between devices with their start and end apart: 2 -> 2, of which waited for: 0 -> 0; matrix products, arithmetic and copies ran while one was open for 0% -> 0% of each run, Pallas kernels for 9% -> 8%
where the time goes in v6:
time: 38.3 us; the launch traced here: 37.9 us
  blocking collectives  21.6 us (56%)
  starting transfers between devices  7.85 us (20%)
  Pallas kernels  6.49 us (17%)
  between operations  1.35 us (4%)
  local copies, waits for them, and re-layouts  0.63 us (2%)
    all_to_all x1, blocking collectives, on_device(): near = lax.all_to_all(sent, 'roll', 0, 0, axis_index_groups=same_core)  12.6 us
    all_to_all x1, blocking collectives, on_device(): pieces = lax.all_to_all(share, 'roll', 0, 0, axis_index_groups=same_core)  8.99 us
    ppermute x1, starting transfers between devices, on_device(): lax.ppermute(near, 'roll', [(rank, rank ^ 1) for rank in range(ranks)])  5.88 us
    pallas_call x1, Pallas kernels, on_device(): pl.pallas_call(attention_kernel, out_shape=(jax.ShapeDtypeStruct((tokens,...  2.55 us
    ppermute x1, starting transfers between devices, on_device(): lax.ppermute(far_share, 'roll', [(rank, rank ^ 1) for rank in range(ranks)])  1.97 us
    pallas_call x1, Pallas kernels, on_device(): pl.pallas_call(finish_kernel, out_shape=(jax.ShapeDtypeStruct((tokens, co...  1.67 us
    pallas_call x1, Pallas kernels, on_device(): pl.pallas_call(near_kernel, out_shape=(pltpu.VMEM((rows, head_size), half...  1.43 us
    pallas_call x1, Pallas kernels, on_device(): pl.pallas_call(spread_kernel, out_shape=(pltpu.VMEM((ranks // 2, owned, 2...  0.79 us
  transfers between devices with their start and end apart: 2, of which 0 were waited for; matrix products, arithmetic and copies ran while one was open for 0% of the time, Pallas kernels for 8%

profile of v6, /device:TPU:1, one launch (start us, length us, event | category | flops | bytes accessed | tf_op | source)
XLA Modules:
  0.0 37.9 jit_solution(2143929336459119268)
XLA Ops:
  1.3 0.8 %shard_map.118 = (bf16[8,64,256]{2,1,0:T(8,128)(2,1)S(1)}, f32[128,128]{1,0:T(8,128)S(1)}) custom-call(s32[1]{0:T(128)S(6)} %copy.13.length_ref, bf16[64,128]{1,0:T(8,128)(2,1)} %key_hbm.1, bf16[64,128]{1,0:T(8,128)(2,1)} %value_hbm.1), custom_call_target="tpu_custom_call" | custom-call | tf_op jit(solution)/shard_map/pallas_call | solution.py:255
  2.1 12.6 %all_to_all.10.near_ref = bf16[8,64,256]{2,1,0:T(8,128)(2,1)S(1)} all-to-all(bf16[8,64,256]{2,1,0:T(8,128)(2,1)S(1)} %get-tuple-element.23), channel_id=1, replica_groups={{0,8,16,24,32,40,48,56},{4,12,20,28,36,44,52,60},{1,9,17,25,33,41,49,57..., dimensions={0} | all-to-all | bytes 524288 | tf_op jit(solution)/shard_map/all_to_all | solution.py:266
  14.7 5.9 %collective-permute-start = (bf16[8,64,256]{2,1,0:T(8,128)(2,1)S(1)}, bf16[8,64,256]{2,1,0:T(8,128)(2,1)S(1)}, u32[]{:S(2)}, u32[]{:S(2)}) collective-permute-start(bf16[8,64,256]{2,1,0:T(8,128)(2,1)S(1)} %all_to_all.10.near_ref), channel_id=1, source_target_pairs={{0,4},{4,0},{8,12},{12,8},{16,20},{20,16},{24,28},{28,24},{32,36},... | collective-permute-start | bytes 786440 | tf_op jit(solution)/shard_map/ppermute | solution.py:267
  20.6 1.4 %shard_map.119 = (bf16[1024,128]{1,0:T(8,128)(2,1)S(1)}, bf16[128,1024]{1,0:T(8,128)(2,1)S(1)}, bf16[2,128,128]{2,1,0:T(8,128)(2,1)S(1)}, f32[1024,512]{1,0:T(8,128)S(1)}) custom-call(bf16[128,1024]{1,0:T(8,128)(2,1)} %bitcast.10, bf16[128,1024]{1,0:T(8,128)(2,1)} %bitcast.11, bf16[128,128]{1,0:T(8,128)(2,1)} %bitcast.12, bf16[128,128]{1,0:T(8,128)(2,1)} %bitcast.13, ...), custom_call_target="tpu_custom_call" | custom-call | flops 134217728 | bytes 524288 | tf_op jit(solution)/shard_map/pallas_call | solution.py:271
  22.0 0.0 collective-permute-done.far_ref
  22.0 2.6 %shard_map.120 = (bf16[128,1024]{1,0:T(8,128)(2,1)}, bf16[1024,1152]{1,0:T(8,128)(2,1)S(1)}, bf16[1024,1152]{1,0:T(8,128)(2,1)S(1)}, bf16[1024,128]{1,0:T(8,128)...) custom-call(f32[128,128]{1,0:T(8,128)S(1)} %get-tuple-element.22.living_ref, ...), custom_call_target="tpu_custom_call" | custom-call | flops 1509949440 | bytes 4194304 | tf_op jit(solution)/shard_map/pallas_call | solution.py:290
  24.6 2.0 %collective-permute-start.1 = (bf16[8,64,256]{2,1,0:T(8,128)(2,1)S(1)}, bf16[8,64,256]{2,1,0:T(8,128)(2,1)S(1)}, u32[]{:S(2)}, u32[]{:S(2)}) collective-permute-start(bf16[8,64,256]{2,1,0:T(8,128)(2,1)S(1)} %get-tuple-element.37), channel_id=1, source_target_pairs={{0,4},{4,0},{8,12},{12,8},{16,20},{20,16},{24,28},{28,24},{32,36},... | collective-permute-start | bytes 786440 | tf_op jit(solution)/shard_map/ppermute | solution.py:310
  26.5 1.7 %shard_map.121 = (bf16[128,1024]{1,0:T(8,128)(2,1)}, bf16[128,128]{1,0:T(8,128)(2,1)}, bf16[128,128]{1,0:T(8,128)(2,1)}, f32[512,256]{1,0:T(8,128)S(1)}) custom-call(bf16[1024,128]{1,0:T(8,128)(2,1)S(1)} %get-tuple-element.24.query_rows_ref, bf16[1024,1152]{1,0:T(8,128)(2,1)S(1)} %get-tuple-element.29.weights_ref, ...), custom_call_target="tpu_custom_call" | custom-call | flops 603979776 | bytes 4194304 | tf_op jit(solution)/shard_map/pallas_call | solution.py:311
  28.2 0.0 collective-permute-done.1.received_ref
  28.3 9.0 %all_to_all.11 = bf16[8,64,256]{2,1,0:T(8,128)(2,1)S(1)} all-to-all(bf16[8,64,256]{2,1,0:T(8,128)(2,1)S(1)} %shard_map.122), channel_id=1, replica_groups={{0,8,16,24,32,40,48,56},{4,12,20,28,36,44,52,60},{1,9,17,25,33,41,49,57..., dimensions={0} | all-to-all | bytes 524288 | tf_op jit(solution)/shard_map/all_to_all | solution.py:336
  37.3 0.6 %fusion = (f32[64,128]{1,0:T(8,128)}, f32[64,128]{1,0:T(8,128)}) fusion(f32[64,256]{1,0:T(8,128)S(1)} %add_bitcast_fusion), kind=kLoop, calls=%fused_computation.1 | loop fusion | bytes 131072 | tf_op jit(solution)/shard_map/slice | solution.py:346
  (2 shorter events, 0.1 us)
Async XLA Ops:
  14.7 7.3 %collective-permute-start = (bf16[8,64,256]{2,1,0:T(8,128)(2,1)S(1)}, bf16[8,64,256]{2,1,0:T(8,128)(2,1)S(1)}, u32[]{:S(2)}, u32[]{:S(2)}) collective-permute-start(bf16[8,64,256]{2,1,0:T(8,128)(2,1)S(1)} %all_to_all.10.near_ref), channel_id=1, source_target_pairs={{0,4},{4,0},{8,12},{12,8},{16,20},{20,16},{24,28},{28,24},{32,36},... | collective-permute-start | bytes 786440 | tf_op jit(solution)/shard_map/ppermute | solution.py:267
  24.6 3.7 %collective-permute-start.1 = (bf16[8,64,256]{2,1,0:T(8,128)(2,1)S(1)}, bf16[8,64,256]{2,1,0:T(8,128)(2,1)S(1)}, u32[]{:S(2)}, u32[]{:S(2)}) collective-permute-start(bf16[8,64,256]{2,1,0:T(8,128)(2,1)S(1)} %get-tuple-element.37), channel_id=1, source_target_pairs={{0,4},{4,0},{8,12},{12,8},{16,20},{20,16},{24,28},{28,24},{32,36},... | collective-permute-start | bytes 786440 | tf_op jit(solution)/shard_map/ppermute | solution.py:310

commit v7 on v6

--- a/solution.py
+++ b/solution.py
@@ -170,10 +170,11 @@
         if step < count:
             normalise(step)
             grad_weigh(step)
+        if step == count - 1:
+            copy = pltpu.make_async_copy(attended_ref, attended_hbm, sem)
+            copy.start()
         if step > 0:
             grad_score(step - 1)
-    copy = pltpu.make_async_copy(attended_ref, attended_hbm, sem)
-    copy.start()
     query = query_rows_ref[...]
     grad = jnp.concatenate([state[0] for state in states], axis=0)
     grad_rows_ref[...] = grad

time: 38.3 us -> 38.3 us (level)
  no operation moved by 1% of the time
where the time goes in v7:
time: 38.3 us; the launch traced here: 37.9 us
  blocking collectives  21.6 us (56%)
  starting transfers between devices  7.85 us (20%)
  Pallas kernels  6.49 us (17%)
  between operations  1.35 us (4%)
  local copies, waits for them, and re-layouts  0.63 us (2%)
    all_to_all x1, blocking collectives, on_device(): near = lax.all_to_all(sent, 'roll', 0, 0, axis_index_groups=same_core)  12.6 us
    all_to_all x1, blocking collectives, on_device(): pieces = lax.all_to_all(share, 'roll', 0, 0, axis_index_groups=same_core)  8.99 us
    ppermute x1, starting transfers between devices, on_device(): lax.ppermute(near, 'roll', [(rank, rank ^ 1) for rank in range(ranks)])  5.88 us
    pallas_call x1, Pallas kernels, on_device(): pl.pallas_call(attention_kernel, out_shape=(jax.ShapeDtypeStruct((tokens,...  2.55 us
    ppermute x1, starting transfers between devices, on_device(): lax.ppermute(far_share, 'roll', [(rank, rank ^ 1) for rank in range(ranks)])  1.97 us
    pallas_call x1, Pallas kernels, on_device(): pl.pallas_call(finish_kernel, out_shape=(jax.ShapeDtypeStruct((tokens, co...  1.67 us
    pallas_call x1, Pallas kernels, on_device(): pl.pallas_call(near_kernel, out_shape=(pltpu.VMEM((rows, head_size), half...  1.43 us
    pallas_call x1, Pallas kernels, on_device(): pl.pallas_call(spread_kernel, out_shape=(pltpu.VMEM((ranks // 2, owned, 2...  0.79 us
  transfers between devices with their start and end apart: 2, of which 0 were waited for; matrix products, arithmetic and copies ran while one was open for 0% of the time, Pallas kernels for 8%

profile of v7, /device:TPU:1, one launch (start us, length us, event | category | flops | bytes accessed | tf_op | source)
XLA Modules:
  0.0 37.9 jit_solution(2143929336459119268)
XLA Ops:
  1.3 0.8 %shard_map.118 = (bf16[8,64,256]{2,1,0:T(8,128)(2,1)S(1)}, f32[128,128]{1,0:T(8,128)S(1)}) custom-call(s32[1]{0:T(128)S(6)} %copy.13.length_ref, bf16[64,128]{1,0:T(8,128)(2,1)} %key_hbm.1, bf16[64,128]{1,0:T(8,128)(2,1)} %value_hbm.1), custom_call_target="tpu_custom_call" | custom-call | tf_op jit(solution)/shard_map/pallas_call | solution.py:256
  2.1 12.6 %all_to_all.10.near_ref = bf16[8,64,256]{2,1,0:T(8,128)(2,1)S(1)} all-to-all(bf16[8,64,256]{2,1,0:T(8,128)(2,1)S(1)} %get-tuple-element.23), channel_id=1, replica_groups={{0,8,16,24,32,40,48,56},{4,12,20,28,36,44,52,60},{1,9,17,25,33,41,49,57..., dimensions={0} | all-to-all | bytes 524288 | tf_op jit(solution)/shard_map/all_to_all | solution.py:267
  14.7 5.9 %collective-permute-start = (bf16[8,64,256]{2,1,0:T(8,128)(2,1)S(1)}, bf16[8,64,256]{2,1,0:T(8,128)(2,1)S(1)}, u32[]{:S(2)}, u32[]{:S(2)}) collective-permute-start(bf16[8,64,256]{2,1,0:T(8,128)(2,1)S(1)} %all_to_all.10.near_ref), channel_id=1, source_target_pairs={{0,4},{4,0},{8,12},{12,8},{16,20},{20,16},{24,28},{28,24},{32,36},... | collective-permute-start | bytes 786440 | tf_op jit(solution)/shard_map/ppermute | solution.py:268
  20.6 1.4 %shard_map.119 = (bf16[1024,128]{1,0:T(8,128)(2,1)S(1)}, bf16[128,1024]{1,0:T(8,128)(2,1)S(1)}, bf16[2,128,128]{2,1,0:T(8,128)(2,1)S(1)}, f32[1024,512]{1,0:T(8,128)S(1)}) custom-call(bf16[128,1024]{1,0:T(8,128)(2,1)} %bitcast.10, bf16[128,1024]{1,0:T(8,128)(2,1)} %bitcast.11, bf16[128,128]{1,0:T(8,128)(2,1)} %bitcast.12, bf16[128,128]{1,0:T(8,128)(2,1)} %bitcast.13, ...), custom_call_target="tpu_custom_call" | custom-call | flops 134217728 | bytes 524288 | tf_op jit(solution)/shard_map/pallas_call | solution.py:272
  22.0 0.0 collective-permute-done.far_ref
  22.0 2.6 %shard_map.120 = (bf16[128,1024]{1,0:T(8,128)(2,1)}, bf16[1024,1152]{1,0:T(8,128)(2,1)S(1)}, bf16[1024,1152]{1,0:T(8,128)(2,1)S(1)}, bf16[1024,128]{1,0:T(8,128)...) custom-call(f32[128,128]{1,0:T(8,128)S(1)} %get-tuple-element.22.living_ref, ...), custom_call_target="tpu_custom_call" | custom-call | flops 1509949440 | bytes 4194304 | tf_op jit(solution)/shard_map/pallas_call | solution.py:291
  24.6 2.0 %collective-permute-start.1 = (bf16[8,64,256]{2,1,0:T(8,128)(2,1)S(1)}, bf16[8,64,256]{2,1,0:T(8,128)(2,1)S(1)}, u32[]{:S(2)}, u32[]{:S(2)}) collective-permute-start(bf16[8,64,256]{2,1,0:T(8,128)(2,1)S(1)} %get-tuple-element.37), channel_id=1, source_target_pairs={{0,4},{4,0},{8,12},{12,8},{16,20},{20,16},{24,28},{28,24},{32,36},... | collective-permute-start | bytes 786440 | tf_op jit(solution)/shard_map/ppermute | solution.py:311
  26.5 1.7 %shard_map.121 = (bf16[128,1024]{1,0:T(8,128)(2,1)}, bf16[128,128]{1,0:T(8,128)(2,1)}, bf16[128,128]{1,0:T(8,128)(2,1)}, f32[512,256]{1,0:T(8,128)S(1)}) custom-call(bf16[1024,128]{1,0:T(8,128)(2,1)S(1)} %get-tuple-element.24.query_rows_ref, bf16[1024,1152]{1,0:T(8,128)(2,1)S(1)} %get-tuple-element.29.weights_ref, ...), custom_call_target="tpu_custom_call" | custom-call | flops 603979776 | bytes 4194304 | tf_op jit(solution)/shard_map/pallas_call | solution.py:312
  28.2 0.0 collective-permute-done.1.received_ref
  28.3 9.0 %all_to_all.11 = bf16[8,64,256]{2,1,0:T(8,128)(2,1)S(1)} all-to-all(bf16[8,64,256]{2,1,0:T(8,128)(2,1)S(1)} %shard_map.122), channel_id=1, replica_groups={{0,8,16,24,32,40,48,56},{4,12,20,28,36,44,52,60},{1,9,17,25,33,41,49,57..., dimensions={0} | all-to-all | bytes 524288 | tf_op jit(solution)/shard_map/all_to_all | solution.py:337
  37.3 0.6 %fusion = (f32[64,128]{1,0:T(8,128)}, f32[64,128]{1,0:T(8,128)}) fusion(f32[64,256]{1,0:T(8,128)S(1)} %add_bitcast_fusion), kind=kLoop, calls=%fused_computation.1 | loop fusion | bytes 131072 | tf_op jit(solution)/shard_map/slice | solution.py:347
  (2 shorter events, 0.1 us)
Async XLA Ops:
  14.7 7.3 %collective-permute-start = (bf16[8,64,256]{2,1,0:T(8,128)(2,1)S(1)}, bf16[8,64,256]{2,1,0:T(8,128)(2,1)S(1)}, u32[]{:S(2)}, u32[]{:S(2)}) collective-permute-start(bf16[8,64,256]{2,1,0:T(8,128)(2,1)S(1)} %all_to_all.10.near_ref), channel_id=1, source_target_pairs={{0,4},{4,0},{8,12},{12,8},{16,20},{20,16},{24,28},{28,24},{32,36},... | collective-permute-start | bytes 786440 | tf_op jit(solution)/shard_map/ppermute | solution.py:268
  24.6 3.7 %collective-permute-start.1 = (bf16[8,64,256]{2,1,0:T(8,128)(2,1)S(1)}, bf16[8,64,256]{2,1,0:T(8,128)(2,1)S(1)}, u32[]{:S(2)}, u32[]{:S(2)}) collective-permute-start(bf16[8,64,256]{2,1,0:T(8,128)(2,1)S(1)} %get-tuple-element.37), channel_id=1, source_target_pairs={{0,4},{4,0},{8,12},{12,8},{16,20},{20,16},{24,28},{28,24},{32,36},... | collective-permute-start | bytes 786440 | tf_op jit(solution)/shard_map/ppermute | solution.py:311

commit v8 on v6

--- a/solution.py
+++ b/solution.py
@@ -25,38 +25,24 @@
     ]
 
 
-def spread_kernel(length_ref, key_hbm, value_hbm, out_ref, living_ref, own, sems):
-    head_size = key_hbm.shape[1]
-    copies = [
-        pltpu.make_async_copy(source, own.at[place], sems.at[place])
-        for place, source in enumerate((key_hbm, value_hbm))
-    ]
-    for copy in copies:
-        copy.start()
-    token = lax.broadcasted_iota(jnp.int32, living_ref.shape, 0)
-    living_ref[...] = (token < length_ref[0]).astype(jnp.float32)
-    for copy in copies:
-        copy.wait()
-    for place in range(out_ref.shape[0]):
-        out_ref[place, :, :head_size] = own[0]
-        out_ref[place, :, head_size:] = own[1]
-
-
-def near_kernel(
+def spread_kernel(
+    key_hbm,
+    value_hbm,
     query_hbm,
     grad_hbm,
     resp_key_hbm,
     resp_value_hbm,
-    near_ref,
-    query_rows_ref,
+    out_ref,
+    query_ref,
     grad_ref,
     own_ref,
-    scores_ref,
-    query_ref,
+    prompt_own,
     sems,
 ):
-    tokens, head_size = own_ref.shape[1:]
+    head_size = key_hbm.shape[1]
     moves = (
+        (key_hbm, prompt_own.at[0]),
+        (value_hbm, prompt_own.at[1]),
         (query_hbm, query_ref),
         (grad_hbm, grad_ref),
         (resp_key_hbm, own_ref.at[0]),
@@ -68,14 +54,25 @@
     ]
     for copy in copies:
         copy.start()
+    for copy in copies[:2]:
+        copy.wait()
+    for place in range(out_ref.shape[0]):
+        out_ref[place, :, :head_size] = prompt_own[0]
+        out_ref[place, :, head_size:] = prompt_own[1]
+    for copy in copies[2:]:
+        copy.wait()
+
+
+def near_kernel(length_ref, query_ref, near_ref, query_rows_ref, scores_ref, living_ref):
+    tokens = query_ref.shape[0]
+    head_size = query_rows_ref.shape[1]
+    token = lax.broadcasted_iota(jnp.int32, living_ref.shape, 0)
+    living_ref[...] = (token < length_ref[0]).astype(jnp.float32)
     keys = jnp.concatenate([near_ref[place, :, :head_size] for place in range(near_ref.shape[0])], axis=0)
-    copies[0].wait()
     for rows, span in head_parts(query_ref.shape[1], tokens, head_size):
         query = query_ref[:, span]
         query_rows_ref[rows] = query
         scores_ref[rows] = contract(query, keys, (1, 1))
-    for copy in copies[1:]:
-        copy.wait()
 
 
 def attention_kernel(
@@ -252,38 +249,39 @@
     vmem = pl.BlockSpec(memory_space=pltpu.VMEM)
     anywhere = pl.BlockSpec(memory_space=pl.ANY)
 
-    sent, living = pl.pallas_call(
+    hbm = pl.BlockSpec(memory_space=pltpu.HBM)
+    stored = (prefix_keys, prefix_values, queries[0], grad_out[0], resp_keys[0], resp_values[0])
+    sent, query, grads, own = pl.pallas_call(
         spread_kernel,
         out_shape=(
             pltpu.VMEM((ranks // 2, owned, 2 * head_size), half),
-            pltpu.VMEM((tokens, head_size), jnp.float32),
-        ),
-        in_specs=[pl.BlockSpec(memory_space=pltpu.SMEM)] + [pl.BlockSpec(memory_space=pltpu.HBM)] * 2,
-        out_specs=[vmem] * 2,
-        scratch_shapes=[pltpu.VMEM((2, owned, head_size), half), pltpu.SemaphoreType.DMA((2,))],
-    )(lengths, *(pltpu.with_memory_space_constraint(array, pltpu.HBM) for array in (prefix_keys, prefix_values)))
+            pltpu.VMEM((tokens, columns), half),
+            pltpu.VMEM((tokens, columns), half),
+            pltpu.VMEM((2, tokens, head_size), half),
+        ),
+        in_specs=[hbm] * 6,
+        out_specs=[vmem] * 4,
+        scratch_shapes=[pltpu.VMEM((2, owned, head_size), half), pltpu.SemaphoreType.DMA((6,))],
+        compiler_params=pltpu.CompilerParams(vmem_limit_bytes=8 * 1024 * 1024),
+    )(*(pltpu.with_memory_space_constraint(array, pltpu.HBM) for array in stored))
     same_core = [list(range(core, ranks, 2)) for core in range(2)]
     near = lax.all_to_all(sent, "roll", 0, 0, axis_index_groups=same_core)
     far = lax.ppermute(near, "roll", [(rank, rank ^ 1) for rank in range(ranks)])
     rows = columns // head_size * tokens
-    hbm = pl.BlockSpec(memory_space=pltpu.HBM)
-    stored = (queries[0], grad_out[0], resp_keys[0], resp_values[0])
-    query_rows, grads, own, near_scores = pl.pallas_call(
+    query_rows, near_scores, living = pl.pallas_call(
         near_kernel,
         out_shape=(
             pltpu.VMEM((rows, head_size), half),
-            pltpu.VMEM((tokens, columns), half),
-            pltpu.VMEM((2, tokens, head_size), half),
             pltpu.VMEM((rows, ranks * owned // 2), jnp.float32),
-        ),
-        in_specs=[hbm] * 4 + [vmem],
-        out_specs=[vmem] * 4,
-        scratch_shapes=[pltpu.VMEM((tokens, columns), half), pltpu.SemaphoreType.DMA((4,))],
+            pltpu.VMEM((tokens, head_size), jnp.float32),
+        ),
+        in_specs=[pl.BlockSpec(memory_space=pltpu.SMEM)] + [vmem] * 2,
+        out_specs=[vmem] * 3,
         compiler_params=pltpu.CompilerParams(vmem_limit_bytes=24 * 1024 * 1024),
         cost_estimate=pl.CostEstimate(
             flops=rows * ranks * owned * head_size, bytes_accessed=4 * rows * head_size, transcendentals=0
         ),
-    )(*(pltpu.with_memory_space_constraint(array, pltpu.HBM) for array in stored), near)
+    )(lengths, query, near)
     limit = pltpu.CompilerParams(vmem_limit_bytes=40 * 1024 * 1024)
     unit = 2 * rows * key_count * head_size
     chips = ranks // 2

time: 38.3 us -> 38.5 us (level)
  Pallas kernels: 6.49 us -> 5.82 us
  blocking collectives: 21.6 us -> 22.2 us
    pallas_call x1, Pallas kernels: 1.43 us -> 0.43 us  [on_device(): pl.pallas_call(near_kernel, out_shape=(pltpu.VMEM((rows, head_size), half...]
    all_to_all x1, blocking collectives: 8.99 us -> 9.58 us  [on_device(): pieces = lax.all_to_all(share, 'roll', 0, 0, axis_index_groups=same_core)]
  transfers between devices with their start and end apart: 2 -> 2, of which waited for: 0 -> 1; matrix products, arithmetic and copies ran while one was open for 0% -> 0% of each run, Pallas kernels for 8% -> 6%
where the time goes in v8:
time: 38.5 us; the launch traced here: 38.2 us
  blocking collectives  22.2 us (58%)
  starting transfers between devices  8.17 us (21%)
  Pallas kernels  5.82 us (15%)
  between operations  1.35 us (4%)
  local copies, waits for them, and re-layouts  0.63 us (2%)
    all_to_all x1, blocking collectives, on_device(): near = lax.all_to_all(sent, 'roll', 0, 0, axis_index_groups=same_core)  12.6 us
    all_to_all x1, blocking collectives, on_device(): pieces = lax.all_to_all(share, 'roll', 0, 0, axis_index_groups=same_core)  9.58 us
    ppermute x1, starting transfers between devices, on_device(): lax.ppermute(near, 'roll', [(rank, rank ^ 1) for rank in range(ranks)])  5.88 us
    pallas_call x1, Pallas kernels, on_device(): pl.pallas_call(attention_kernel, out_shape=(jax.ShapeDtypeStruct((tokens,...  2.55 us
    ppermute x1, starting transfers between devices, on_device(): lax.ppermute(far_share, 'roll', [(rank, rank ^ 1) for rank in range(ranks)])  2.28 us
    pallas_call x1, Pallas kernels, on_device(): pl.pallas_call(finish_kernel, out_shape=(jax.ShapeDtypeStruct((tokens, co...  1.67 us
    pallas_call x1, Pallas kernels, on_device(): pl.pallas_call(spread_kernel, out_shape=(pltpu.VMEM((ranks // 2, owned, 2...  1.12 us
  transfers between devices with their start and end apart: 2, of which 1 were waited for; matrix products, arithmetic and copies ran while one was open for 0% of the time, Pallas kernels for 6%

profile of v8, /device:TPU:1, one launch (start us, length us, event | category | flops | bytes accessed | tf_op | source)
XLA Modules:
  0.0 38.2 jit_solution(13802130387816076778)
XLA Ops:
  0.6 1.1 %shard_map.118 = (bf16[8,64,256]{2,1,0:T(8,128)(2,1)S(1)}, bf16[128,1024]{1,0:T(8,128)(2,1)S(1)}, bf16[128,1024]{1,0:T(8,128)(2,1)S(1)}, bf16[2,128,128]{2,1,0:T(8,128)(2,1)S(1)}) custom-call(bf16[64,128]{1,0:T(8,128)(2,1)} %key_hbm.1, bf16[64,128]{1,0:T(8,128)(2,1)} %value_hbm.1, bf16[128,1024]{1,0:T(8,128)(2,1)} %bitcast.10, bf16[128,1024]{1,0:T(8,128)(2,1)} %bitcast.11, ...), custom_call_target="tpu_custom_call" | custom-call | tf_op jit(solution)/shard_map/pallas_call | solution.py:254
  1.8 12.6 %all_to_all.10.near_ref = bf16[8,64,256]{2,1,0:T(8,128)(2,1)S(1)} all-to-all(bf16[8,64,256]{2,1,0:T(8,128)(2,1)S(1)} %get-tuple-element.24), channel_id=1, replica_groups={{0,8,16,24,32,40,48,56},{4,12,20,28,36,44,52,60},{1,9,17,25,33,41,49,57..., dimensions={0} | all-to-all | bytes 524288 | tf_op jit(solution)/shard_map/all_to_all | solution.py:268
  14.4 5.9 %collective-permute-start = (bf16[8,64,256]{2,1,0:T(8,128)(2,1)S(1)}, bf16[8,64,256]{2,1,0:T(8,128)(2,1)S(1)}, u32[]{:S(2)}, u32[]{:S(2)}) collective-permute-start(bf16[8,64,256]{2,1,0:T(8,128)(2,1)S(1)} %all_to_all.10.near_ref), channel_id=1, source_target_pairs={{0,4},{4,0},{8,12},{12,8},{16,20},{20,16},{24,28},{28,24},{32,36},... | collective-permute-start | bytes 786440 | tf_op jit(solution)/shard_map/ppermute | solution.py:269
  20.9 0.4 %shard_map.119 = (bf16[1024,128]{1,0:T(8,128)(2,1)S(1)}, f32[1024,512]{1,0:T(8,128)S(1)}, f32[128,128]{1,0:T(8,128)S(1)}) custom-call(s32[1]{0:T(128)S(6)} %copy.13.length_ref, bf16[128,1024]{1,0:T(8,128)(2,1)S(1)} %get-tuple-element.23.query_ref, bf16[8,64,256]{2,1,0:T(8,128)(2,1)S(1)} %all_to_all.10.near_ref), custom_call_target="tpu_custom_call" | custom-call | flops 134217728 | bytes 524288 | tf_op jit(solution)/shard_map/pallas_call | solution.py:271
  21.3 0.1 collective-permute-done.far_ref
  21.4 2.5 %shard_map.120 = (bf16[128,1024]{1,0:T(8,128)(2,1)}, bf16[1024,1152]{1,0:T(8,128)(2,1)S(1)}, bf16[1024,1152]{1,0:T(8,128)(2,1)S(1)}, bf16[1024,128]{1,0:T(8,128)...) custom-call(f32[128,128]{1,0:T(8,128)S(1)} %get-tuple-element.25.living_ref, ...), custom_call_target="tpu_custom_call" | custom-call | flops 1509949440 | bytes 4194304 | tf_op jit(solution)/shard_map/pallas_call | solution.py:288
  23.9 2.3 %collective-permute-start.1 = (bf16[8,64,256]{2,1,0:T(8,128)(2,1)S(1)}, bf16[8,64,256]{2,1,0:T(8,128)(2,1)S(1)}, u32[]{:S(2)}, u32[]{:S(2)}) collective-permute-start(bf16[8,64,256]{2,1,0:T(8,128)(2,1)S(1)} %get-tuple-element.39), channel_id=1, source_target_pairs={{0,4},{4,0},{8,12},{12,8},{16,20},{20,16},{24,28},{28,24},{32,36},... | collective-permute-start | bytes 786440 | tf_op jit(solution)/shard_map/ppermute | solution.py:308
  26.2 1.7 %shard_map.121 = (bf16[128,1024]{1,0:T(8,128)(2,1)}, bf16[128,128]{1,0:T(8,128)(2,1)}, bf16[128,128]{1,0:T(8,128)(2,1)}, f32[512,256]{1,0:T(8,128)S(1)}) custom-call(bf16[1024,128]{1,0:T(8,128)(2,1)S(1)} %get-tuple-element.26.query_rows_ref, bf16[1024,1152]{1,0:T(8,128)(2,1)S(1)} %get-tuple-element.31.weights_ref, ...), custom_call_target="tpu_custom_call" | custom-call | flops 603979776 | bytes 4194304 | tf_op jit(solution)/shard_map/pallas_call | solution.py:309
  27.9 0.0 collective-permute-done.1.received_ref
  28.0 9.6 %all_to_all.11 = bf16[8,64,256]{2,1,0:T(8,128)(2,1)S(1)} all-to-all(bf16[8,64,256]{2,1,0:T(8,128)(2,1)S(1)} %shard_map.122), channel_id=1, replica_groups={{0,8,16,24,32,40,48,56},{4,12,20,28,36,44,52,60},{1,9,17,25,33,41,49,57..., dimensions={0} | all-to-all | bytes 524288 | tf_op jit(solution)/shard_map/all_to_all | solution.py:334
  37.6 0.6 %fusion = (f32[64,128]{1,0:T(8,128)}, f32[64,128]{1,0:T(8,128)}) fusion(f32[64,256]{1,0:T(8,128)S(1)} %add_bitcast_fusion), kind=kLoop, calls=%fused_computation.1 | loop fusion | bytes 131072 | tf_op jit(solution)/shard_map/slice | solution.py:344
  (2 shorter events, 0.1 us)
Async XLA Ops:
  14.4 7.0 %collective-permute-start = (bf16[8,64,256]{2,1,0:T(8,128)(2,1)S(1)}, bf16[8,64,256]{2,1,0:T(8,128)(2,1)S(1)}, u32[]{:S(2)}, u32[]{:S(2)}) collective-permute-start(bf16[8,64,256]{2,1,0:T(8,128)(2,1)S(1)} %all_to_all.10.near_ref), channel_id=1, source_target_pairs={{0,4},{4,0},{8,12},{12,8},{16,20},{20,16},{24,28},{28,24},{32,36},... | collective-permute-start | bytes 786440 | tf_op jit(solution)/shard_map/ppermute | solution.py:269
  23.9 4.0 %collective-permute-start.1 = (bf16[8,64,256]{2,1,0:T(8,128)(2,1)S(1)}, bf16[8,64,256]{2,1,0:T(8,128)(2,1)S(1)}, u32[]{:S(2)}, u32[]{:S(2)}) collective-permute-start(bf16[8,64,256]{2,1,0:T(8,128)(2,1)S(1)} %get-tuple-element.39), channel_id=1, source_target_pairs={{0,4},{4,0},{8,12},{12,8},{16,20},{20,16},{24,28},{28,24},{32,36},... | collective-permute-start | bytes 786440 | tf_op jit(solution)/shard_map/ppermute | solution.py:308
